TPU v7x, 32 devices: a whole 2x2x4 slice. The times are simulated.
32 devices in a mesh: dp: 32 (over z, y, x, core).
Axes of the slice: x: 2, y: 2, z: 4, core: 2. Of those that a mesh axis runs over, the one named last changes fastest.
Arguments:
- frames: bfloat16 [16384, 768], P('dp'), may hold values from -6 to 6
- ln1_gain: bfloat16 [768], P('dp'), may hold values from 0.5 to 1.5
- ln1_shift: bfloat16 [768], P('dp'), may hold values from -1.75 to 1.75
- w_query: bfloat16 [768, 768], P('dp'), may hold values from -0.21875 to 0.21875
- b_query: bfloat16 [768], P('dp'), may hold values from -3 to 3
- w_key: bfloat16 [768, 768], P('dp'), may hold values from -0.21875 to 0.21875
- w_value: bfloat16 [768, 768], P('dp'), may hold values from -0.21875 to 0.21875
- b_value: bfloat16 [768], P('dp'), may hold values from -1.75 to 1.75
- w_out: bfloat16 [768, 768], P('dp'), may hold values from -2.5 to 2.5
- b_out: bfloat16 [768], P('dp'), may hold values from -1.75 to 1.75
- ln2_gain: bfloat16 [768], P('dp'), may hold values from 0.5 to 1.5
- ln2_shift: bfloat16 [768], P('dp'), may hold values from -1.75 to 1.75
- w_inner: bfloat16 [768, 3072], P('dp'), may hold values from -0.21875 to 0.21875
- b_inner: bfloat16 [3072], P('dp'), may hold values from -3 to 3
- w_outer: bfloat16 [3072, 768], P('dp'), may hold values from -0.109375 to 0.109375
- b_outer: bfloat16 [768], P('dp'), may hold values from -1.75 to 1.75
- bias_table: bfloat16 [3840], P('dp'), may hold values from -6 to 6
- layout: int32 [32], P('dp'), may hold values from 0 to 3, as said below
- valid: int32 [32, 4], P('dp'), may hold values from 65 to 384, as said below
- rel_index: int32 [1023], replicated, may hold values from 0 to 319
- cotangent: bfloat16 [16384, 768], P('dp'), may hold values from -6 to 6
Outputs:
- mixed: bfloat16 [16384, 768], P('dp')
- frames_grad: bfloat16 [16384, 768], P('dp')
- grad_ln1_gain: float32 [768], P('dp')
- grad_ln1_shift: float32 [768], P('dp')
- grad_w_query: float32 [768, 768], P('dp')
- grad_b_query: float32 [768], P('dp')
- grad_w_key: float32 [768, 768], P('dp')
- grad_w_value: float32 [768, 768], P('dp')
- grad_b_value: float32 [768], P('dp')
- grad_w_out: float32 [768, 768], P('dp')
- grad_b_out: float32 [768], P('dp')
- grad_ln2_gain: float32 [768], P('dp')
- grad_ln2_shift: float32 [768], P('dp')
- grad_w_inner: float32 [768, 3072], P('dp')
- grad_b_inner: float32 [3072], P('dp')
- grad_w_outer: float32 [3072, 768], P('dp')
- grad_b_outer: float32 [768], P('dp')
- grad_bias_table: float32 [3840], P('dp')
Inputs may be any that keep to these rules, and one draw needn't show every extreme that they name: `layout`: every code 0 to 3 is taken by some group in every draw. For the s-th sequence of a group, valid holds more than half of its length and at most its length; entries of slots past a group's last sequence are ignored. Some sequence of 384 frames is valid in full in every draw.
All inputs are finite; a program needn't handle non-finite values.
Results may differ from a plain program's by a relative error of at most 0.013.
Values may be sent and summed in bfloat16 or wider, within the bound.
No kernel may reach another device: no remote copies, remote signals or barrier semaphores. Data moves between devices by JAX's collectives and lax.ppermute only.
A program may use at most 192 MiB of HBM per device.

v0:
```python
import functools
import math

import jax
import jax.numpy as jnp
import numpy as np
from jax import lax
from jax.experimental import pallas as pl
from jax.experimental.pallas import tpu as pltpu
from jax.sharding import PartitionSpec as P

HEADS = 12
LANES = 128
UNITS = 4
MASKED = -1e30
F32 = jnp.float32
BF16 = jnp.bfloat16
SEGMENT = ((0, 0, 0, 1), (0, 0, 1, 1), (0, 0, 1, 2), (0, 1, 2, 3))
START = ((0, 0, 0, 3), (0, 0, 2, 2), (0, 0, 2, 3), (0, 1, 2, 3))
MIB = 1024 * 1024
COUNTS = (3, 3)


def bit_orders(n, kind):
    chip = [1 << k for k in range(1, n.bit_length() - 1)]
    low, high = chip[:2], chip[2:][::-1]
    if kind == "outer":
        return (low[:1] + high + low[1:], low[1:] + high + low[:1])
    return (high + low, high + low[::-1])


def gather_masks(bits):
    masks = [0]
    for bit in bits:
        masks = masks + [bit ^ m for m in masks]
    return masks


def scatter_masks(bits):
    masks = [0]
    for bit in bits:
        masks = [bit ^ m for m in masks] + masks
    return masks


def pairs(n, by_core):
    return [(i, i ^ by_core[i & 1]) for i in range(n)]


class Order:
    def __init__(self):
        self.last = None

    def after(self, *arrays):
        if self.last is None:
            return arrays
        return lax.optimization_barrier((*arrays, self.last))[:-1]

    def did(self, array):
        self.last = array


class Gather:
    def __init__(self, part, n, order, kind="inner"):
        self.n = n
        self.order = order
        self.steps = list(zip(*bit_orders(n, kind)))
        self.held = part if part.ndim == 3 else part[None]
        self.got = lax.ppermute(self.held, "dp", pairs(n, self.steps.pop(0)))

    def step(self):
        pair = self.order.after(self.held, self.got)
        self.held = jnp.concatenate(pair, axis=0)
        self.order.did(self.held)
        self.got = lax.ppermute(self.held, "dp", pairs(self.n, self.steps.pop(0)))
        return self

    def finish(self):
        while self.steps:
            self.step()
        (self.got,) = self.order.after(self.got)
        swap = pairs(self.n, (1, 1))
        return (self.held, self.got, lax.ppermute(self.held, "dp", swap), lax.ppermute(self.got, "dp", swap))


class Scatter:
    def __init__(self, n, order, kind="inner"):
        self.n = n
        self.order = order
        self.parts = []
        self.terms = []
        self.at = 0
        self.steps = list(reversed(list(zip(*bit_orders(n, kind)))))
        self.half = n // 4

    def add(self, send, keep):
        self.parts.append((keep, lax.ppermute(send, "dp", pairs(self.n, (1, 1)))))
        return self

    def total(self, count, dtype):
        at = self.at
        held = [(t, first) for t, first in self.terms if first <= at and at + count <= first + t.shape[0]]
        flat = [t for part in self.parts for t in part] + [t for t, _ in held]
        flat = list(self.order.after(*flat))
        cut = [lax.slice_in_dim(t, at, at + count).astype(F32) for t in flat[: 2 * len(self.parts)]]
        out = [cut[2 * i] + cut[2 * i + 1] for i in range(len(self.parts))]
        out = out[0] if len(out) == 1 else jnp.concatenate(out, axis=-1)
        for t, (_, first) in zip(flat[2 * len(self.parts) :], held):
            out = out + lax.slice_in_dim(t, at - first, at - first + count).astype(F32)
        out = out.astype(dtype)
        self.order.did(out)
        return out

    def step(self, transfers=1):
        by_core = self.steps.pop(0)
        count = self.half // transfers
        for _ in range(transfers):
            out = self.total(count, BF16)
            self.terms.append((lax.ppermute(out, "dp", pairs(self.n, by_core)), self.at + self.half))
            self.at += count
        self.half //= 2

    def finish(self):
        while self.steps:
            self.step()
        return self.total(1, F32)[0]


def plan_tables(n, kind="inner"):
    orders = bit_orders(n, kind)
    me = lax.axis_index("dp")
    core = me & 1
    g = np.array([gather_masks(o) for o in orders], np.int32)
    s = np.array([scatter_masks(o) for o in orders], np.int32)
    inverse = np.zeros((2, n), np.int32)
    for c in (0, 1):
        for i, m in enumerate(s[c]):
            inverse[c, m] = i
    devices = jnp.arange(n, dtype=jnp.int32)
    chips = (me ^ jnp.where(core == 0, jnp.asarray(g[0]), jnp.asarray(g[1]))) >> 1
    mask = (devices ^ me) & ~1
    place = jnp.sum(jnp.where(mask[:, None] == devices[None, :], jnp.asarray(inverse)[np.arange(n) % 2], 0), axis=1)
    return core, chips, place


def crossed_places(n, kind="inner"):
    first, second = (gather_masks(o) for o in bit_orders(n, kind))
    places = [second.index(m) for m in first]
    assert places == [first.index(m) for m in second]
    return places


def gathered(parts, plan, n):
    core, chips, _ = plan
    mine = jnp.concatenate(parts[:2])
    theirs = jnp.concatenate(parts[2:])[np.array(crossed_places(n))]
    both = jnp.where(core == 0, jnp.stack([mine, theirs], 1), jnp.stack([theirs, mine], 1))
    return both[jnp.argsort(chips)].reshape(n * mine.shape[1], mine.shape[2])


def split_natural(grad, plan, n):
    core, _, place = plan
    rows = grad.shape[0] // n
    blocks = grad.reshape(n // 2, 2, rows, grad.shape[1])
    mine = jnp.where(core == 0, blocks[:, 0], blocks[:, 1])
    theirs = jnp.where(core == 0, blocks[:, 1], blocks[:, 0])
    both = place.reshape(n // 2, 2)
    my_place = jnp.where(core == 0, both[:, 0], both[:, 1])
    their_place = jnp.where(core == 0, both[:, 1], both[:, 0])
    return theirs[jnp.argsort(their_place)], mine[jnp.argsort(my_place)]


def nn(a, b):
    return jnp.dot(a, b, preferred_element_type=F32)


def nt(a, b):
    return lax.dot_general(a, b, (((1,), (1,)), ((), ())), preferred_element_type=F32)


def tn(a, b):
    return lax.dot_general(a, b, (((0,), (0,)), ((), ())), preferred_element_type=F32)


def normalise(v):
    centred = v - jnp.mean(v, axis=-1, keepdims=True)
    r = lax.rsqrt(jnp.mean(centred * centred, axis=-1, keepdims=True) + 1e-05)
    return centred * r, r


def norm_backward(n, r, gain, e):
    eg = e * gain
    return r * (eg - jnp.mean(eg, axis=-1, keepdims=True) - n * jnp.mean(eg * n, axis=-1, keepdims=True))


def pick(table, code, u):
    out = jnp.int32(table[0][u])
    for c in range(1, 4):
        out = jnp.where(code == c, jnp.int32(table[c][u]), out)
    return out


def unit_range(meta, u, unit):
    code = meta[0]
    segment = pick(SEGMENT, code, u)
    start = pick(START, code, u)
    count = meta[1]
    for s in range(1, 4):
        count = jnp.where(segment == s, meta[1 + s], count)
    window = jnp.minimum(start, 1) * unit
    return start * unit, start * unit + count, window


def put_masks(meta, masks):
    units, window, unit = masks.shape
    row_at = lax.broadcasted_iota(jnp.int32, (window, unit), 0)
    starts = []
    for u in range(units):
        first, end, start = unit_range(meta, u, unit)
        masks[u] = jnp.where((row_at + start >= first) & (row_at + start < end), 0.0, MASKED)
        starts.append(start)
    return starts


def skewed(row, unit):
    wide = jnp.broadcast_to(row, (unit, row.shape[1]))
    return pltpu.roll(wide, row.shape[1] - (unit - 1), 1, stride=1, stride_axis=0)


def unskewed_sum(block, unit):
    width = block.shape[1]
    total = None
    for a in range(unit // 8):
        part = block[8 * a : 8 * a + 8]
        shift = (unit - 1 - 8 * a) % width
        part = pltpu.roll(part, shift, 1) if shift else part
        total = part if total is None else total + part
    out = total[0:1]
    for s in range(1, 8):
        out = out + pltpu.roll(total[s : s + 1], width - s, 1)
    return out


def unpack(core, chips, parts, crossed, out, columns):
    half = parts[0].shape[0]
    for i, j in enumerate(crossed):
        mine = parts[i // half][i % half, :, columns]
        theirs = parts[2 + j // half][j % half, :, columns]
        first = jnp.where(core == 0, mine, theirs)
        second = jnp.where(core == 0, theirs, mine)
        out[chips[i]] = jnp.concatenate([first, second], axis=0)


def weight(ref, columns):
    value = ref[..., columns]
    return value.reshape(-1, value.shape[-1])


def put_blocks(core, places, blocks, send, keep, columns):
    for plane in range(2):

        @pl.when(core == plane)
        def _(plane=plane):
            for at, (place, block) in enumerate(zip(places, blocks)):
                (keep if at % 2 == plane else send)[place, :, columns] = block.astype(BF16)


def row_blocks(value, rows):
    return [value[at : at + rows] for at in range(0, value.shape[0], rows)]


def project_body(meta, frames, w, vec, q_out, k_out, v_out, nin_out):
    width = frames.shape[1]
    head = width // HEADS
    n, _ = normalise(frames[...].astype(F32))
    nin = (n * vec[0:1, :] + vec[1:2, :]).astype(BF16)
    nin_out[...] = nin
    q_out[...] = ((nn(nin, weight(w, slice(0, width))) + vec[2:3, :]) * (head**-0.5)).astype(BF16)
    k_out[...] = nn(nin, weight(w, slice(width, 2 * width))).astype(BF16)
    v_out[...] = (nn(nin, weight(w, slice(2 * width, 3 * width))) + vec[3:4, :]).astype(BF16)


def apart_heads(rows, lane, head):
    zero = jnp.zeros_like(rows)
    return jnp.concatenate([jnp.where(lane < head, rows, zero), jnp.where(lane < head, zero, rows)], axis=0)


def attend_kernel(meta, q, k, v, bias_rev, ctx_out, lse_out, base, vt, masks):
    rows, width = q.shape
    unit = rows // UNITS
    window = rows - unit
    head = width // HEADS
    ranges = put_masks(meta, masks)
    lane = lax.broadcasted_iota(jnp.int32, (unit, LANES), 1)
    sub_lane = lax.broadcasted_iota(jnp.int32, (LANES, unit), 0)

    def pair(hp, carry):
        cols = pl.ds(pl.multiple_of(hp * LANES, LANES), LANES)
        vt[...] = jnp.transpose(v[:, cols])
        for sub in range(2):
            base[sub] = skewed(bias_rev[pl.ds(2 * hp + sub, 1), :], unit)
        for u in range(UNITS):
            ws = pl.multiple_of(ranges[u], LANES)
            win = pl.ds(ws, window)
            urows = slice(u * unit, (u + 1) * unit)
            kk = k[win, cols]
            qu = q[urows, cols]
            offsets = [
                pl.ds(pl.multiple_of((rows - unit) + u * unit - ws - jb * unit, LANES), unit) for jb in range(UNITS - 1)
            ]
            parts = []
            for sub in range(2):
                qs = jnp.where((lane >= head) == bool(sub), qu, jnp.zeros_like(qu))
                rel = jnp.concatenate([base[sub, :, o] for o in offsets], axis=0)
                s = nt(kk, qs) + rel + masks[u]
                top = jnp.max(s, axis=0, keepdims=True)
                e = jnp.exp(s - top)
                tot = jnp.sum(e, axis=0, keepdims=True)
                parts.append(nn(vt[:, win], e.astype(BF16)) * (1.0 / tot))
                lse_out[2 * hp + sub, :, urows] = top + jnp.log(tot)
            ctx_out[urows, cols] = jnp.transpose(jnp.where(sub_lane < head, parts[0], parts[1])).astype(BF16)
        return carry

    lax.fori_loop(0, HEADS // 2, pair, 0)


def small_vectors(core, chips, parts, crossed, at, rows_d, rows_ff, vec3, inner3, table):
    half = parts[0].shape[0]
    lane = lax.broadcasted_iota(jnp.int32, (8, LANES), 1)
    vec3[...] = jnp.zeros_like(vec3)
    inner3[...] = jnp.zeros_like(inner3)
    for i, j in enumerate(crossed):
        mine = parts[i // half][i % half, :, at : at + LANES].astype(F32)
        theirs = parts[2 + j // half][j % half, :, at : at + LANES].astype(F32)
        for plane in range(2):
            block = jnp.where(core == plane, mine, theirs)
            d = 2 * chips[i] + plane
            unit_half = rows_ff // 2
            half_at = 2 * half * rows_ff
            for first, rows, part, out in (
                (0, rows_d, block[0:8], vec3),
                (0, unit_half, block[8:16], inner3),
                (half_at, unit_half, block[16:24], inner3),
            ):
                start = first + d * rows
                tile = start >> 7
                shift = start & (LANES - 1)
                rolled = pltpu.roll(part, shift, 1)
                out[tile] += jnp.where(lane >= shift, rolled, 0.0)
                out[tile + 1] += jnp.where(lane < shift, rolled, 0.0)
            table[pl.ds(d, 1), :] = block[9:10]


def relative_rows(bucket, table, out):
    devices = lax.broadcasted_iota(jnp.int32, (table.shape[0], bucket.shape[1]), 0)
    hot = jnp.where(devices == bucket[0:1, :], 1.0, 0.0).astype(BF16)
    rows = tn(table[...].astype(BF16), hot)
    total = jnp.zeros((HEADS, bucket.shape[1]), F32)
    for m in range(LANES // HEADS):
        total = total + jnp.where(bucket[1:2, :] == m, rows[m * HEADS : (m + 1) * HEADS], 0.0)
    out[0:HEADS, :] = total
    out[HEADS:, :] = jnp.zeros_like(out[HEADS:, :])


def project_kernel(
    meta, frames, p0, p1, p2, p3, bucket_rev,
    q_out, k_out, v_out, nin_out, w, vec, b_inner, bias_rev,
    vec3, inner3, table, *, crossed, rows_d, rows_ff,
):
    width = frames.shape[1]
    core = meta[5]
    chips = [meta[6 + i] for i in range(len(crossed))]
    parts = (p0, p1, p2, p3)
    small_vectors(core, chips, parts, crossed, 3 * width, rows_d, rows_ff, vec3, inner3, table)
    for a in range(width // LANES):
        vec[:, a * LANES : (a + 1) * LANES] = vec3[a]
    for a in range(b_inner.shape[1] // LANES):
        b_inner[:, a * LANES : (a + 1) * LANES] = inner3[a, 0:1]
    relative_rows(bucket_rev, table, bias_rev)
    unpack(core, chips, parts, crossed, w, slice(0, 3 * width))
    project_body(meta, frames, w, vec, q_out, k_out, v_out, nin_out)


def unpack_folded(core, chips, parts, crossed, out, at, width):
    half = parts[0].shape[0]
    for i, j in enumerate(crossed):
        mine = parts[i // half][i % half, :, at : at + 2 * width]
        theirs = parts[2 + j // half][j % half, :, at : at + 2 * width]
        first = jnp.where(core == 0, mine, theirs)
        second = jnp.where(core == 0, theirs, mine)
        rows = [first[:, :width], first[:, width:], second[:, :width], second[:, width:]]
        out[chips[i]] = jnp.concatenate(rows, axis=0)


def feed_tiles(meta, kind, crossed, parts, natural, b_inner, cot, first, nmid, acc, gmid, gb_out, send, keep, w_tile, w_rows, rows_d):
    width = nmid.shape[1]
    tiles = b_inner.shape[1] // width // 2
    if crossed:
        half = len(crossed)
        core = meta[5]
        chips_at = 6 + half * (kind == "outer")
        chips = [meta[chips_at + i] for i in range(half)]
        place_at = 6 + 2 * half + 2 * half * (first == 0)
        place = [meta[place_at + i] for i in range(2 * half)]
        unpack_folded(core, chips, parts, crossed, w_rows, tiles * width, width)
        w_outer = w_rows.reshape(tiles * width, width)
    else:
        w, w_outer = natural

    def tile(t, carry):
        here = pl.multiple_of(t * width, LANES)
        cols = pl.ds(here, width)
        all_cols = pl.ds(pl.multiple_of(first + here, LANES), width)
        if crossed:
            unpack(core, chips, parts, crossed, w_tile, cols)
            wi = weight(w_tile, slice(None))
            wo = w_outer[cols, :]
        else:
            wi = w[:, all_cols]
            wo = w_outer[all_cols, :]
        v = nn(nmid[...], wi) + b_inner[:, all_cols]
        phi = 0.5 * (1.0 + lax.erf(v * (0.5**0.5)))
        act = (v * phi).astype(BF16)
        slope = phi + v * jnp.exp(-0.5 * v * v) * 0.3989422804014327
        acc[...] += nn(act, wo)
        gi = (slope * nt(cot[...], wo)).astype(BF16)
        gb_out[:, cols] = jnp.sum(gi.astype(F32), axis=0, keepdims=True)
        gmid[...] += nt(gi, wi)
        g_outer = tn(act, cot[...])
        g_inner = tn(nmid[...], gi)
        if crossed:
            put_blocks(core, place, row_blocks(g_inner, rows_d), send, keep, cols)
            per = width // (2 * rows_d)
            places = [meta[place_at + t * per + at] for at in range(per)]
            rows = row_blocks(g_outer, rows_d)
            blocks = [jnp.concatenate(rows[2 * at : 2 * at + 2], axis=1) for at in range(per)]
            put_blocks(core, places, blocks, send, keep, slice(tiles * width, (tiles + 2) * width))
        else:
            keep[0, :width, cols] = g_inner.astype(BF16)
            keep[1, cols, :width] = g_outer.astype(BF16)
        return carry

    lax.fori_loop(0, tiles, tile, 0)


def feed_first_kernel(meta, frames, ctx, vec, b_inner, cot, *refs, crossed, rows_d):
    rows, width = frames.shape
    ff = b_inner.shape[1]
    if crossed:
        parts, refs = refs[:4], refs[4:]
        att, nmid, acc, gmid, gb_out, send, keep, w_out, w_tile, w_rows = refs
        chips = [meta[6 + i] for i in range(len(crossed))]
        unpack(meta[5], chips, parts, crossed, w_out, slice(ff, ff + width))
        wo, natural = weight(w_out, slice(None)), None
    else:
        w, w_outer, att, nmid, acc, gmid, gb_out, send, keep = refs
        parts, natural, w_tile, w_rows = None, (w, w_outer), None, None
        wo = w[:, ff : ff + width]
    attended = frames[...].astype(F32) + nn(ctx[...], wo) + vec[4:5, :]
    att[...] = attended
    n, _ = normalise(attended)
    nmid[...] = (n * vec[5:6, :] + vec[6:7, :]).astype(BF16)
    acc[...] = attended + vec[7:8, :]
    gmid[...] = jnp.zeros_like(gmid)
    feed_tiles(
        meta, "inner", crossed, parts, natural, b_inner, cot, 0, nmid, acc, gmid, gb_out, send, keep, w_tile, w_rows, rows_d
    )


def feed_second_kernel(meta, att, nmid, acc_in, gmid_in, ctx, vec, b_inner, cot, *refs, crossed, rows_d):
    rows, width = att.shape
    ff = b_inner.shape[1]
    if crossed:
        w_out, parts, refs = refs[0], refs[1:5], refs[5:]
        mixed_out, gatt_out, gctx_out, send, keep, gb_out, gvec_out, acc, gmid, w_tile, w_rows = refs
        wo, natural = weight(w_out, slice(None)), None
    else:
        w, w_outer, mixed_out, gatt_out, gctx_out, send, keep, gb_out, gvec_out, acc, gmid = refs
        parts, natural, w_tile, w_rows = None, (w, w_outer), None, None
        wo = w[:, ff : ff + width]
    acc[...] = acc_in[...]
    gmid[...] = gmid_in[...]
    feed_tiles(
        meta, "outer", crossed, parts, natural, b_inner, cot, ff // 2, nmid, acc, gmid, gb_out, send, keep, w_tile, w_rows, rows_d
    )
    mixed_out[...] = acc[...].astype(BF16)
    n, r = normalise(att[...])
    e = gmid[...]
    c32 = cot[...].astype(F32)
    gatt = c32 + norm_backward(n, r, vec[5:6, :], e)
    gatt_out[...] = gatt
    gbr = gatt.astype(BF16)
    gctx_out[...] = nt(gbr, wo).astype(BF16)
    gvec_out[0:1, :] = jnp.sum(gbr.astype(F32), axis=0, keepdims=True)
    gvec_out[1:2, :] = jnp.sum(e * n, axis=0, keepdims=True)
    gvec_out[2:3, :] = jnp.sum(e, axis=0, keepdims=True)
    gvec_out[3:4, :] = jnp.sum(c32, axis=0, keepdims=True)
    gvec_out[4:8, :] = jnp.zeros_like(gvec_out[4:8, :])


def moved_lanes(value, moves):
    lane = lax.broadcasted_iota(jnp.int32, (value.shape[0], LANES), 1)
    out = [None] * (value.shape[1] // LANES)
    for source, target, count in moves:
        while count:
            step = min(count, LANES - source % LANES, LANES - target % LANES)
            piece = value[:, source - source % LANES : source - source % LANES + LANES]
            shift = (target - source) % LANES
            piece = pltpu.roll(piece, shift, 1) if shift else piece
            at = target % LANES
            old = out[target // LANES]
            inside = (lane >= at) & (lane < at + step)
            out[target // LANES] = piece if old is None else jnp.where(inside, piece, old)
            source, target, count = source + step, target + step, count - step
    return jnp.concatenate(out, axis=1)


def pack_first_kernel(*refs, rows_ff):
    w_query, w_key, w_value, *vectors, b_inner, table, out, small = refs
    rows, width = w_query.shape
    for i, part in enumerate((w_query, w_key, w_value)):
        out[0, :, i * width : (i + 1) * width] = part[...]
    half = rows_ff // 2
    small[...] = jnp.zeros_like(small)
    for i, vector in enumerate(vectors):
        small[i : i + 1, 0:rows] = vector[...].astype(F32)
    small[8:9, 0:half] = b_inner[:, 0:half].astype(F32)
    small[9:10, 0 : table.shape[1]] = table[...].astype(F32)
    small[16:17, 0:half] = b_inner[:, half:].astype(F32)
    out[0, :, 3 * width :] = small[...].astype(BF16)


def pack_feed_kernel(w_inner, w_outer, w_out, second, third, *, moves):
    rows, width = w_out.shape
    half = w_inner.shape[1] // 2
    inner = moved_lanes(w_inner[...].astype(F32), moves).astype(BF16)
    for part, out in enumerate((second, third)):
        out[0, :, 0:half] = inner[:, part * half : (part + 1) * half]
        for i in range(2):
            at = (2 * part + i) * rows
            out[0, :, half + i * width : half + (i + 1) * width] = w_outer[at : at + rows, :]
    second[0, :, 2 * half :] = w_out[...]


def columns_kernel(early, late, q_out, k_out, v_out, inner_out, table_out, *vectors, counts):
    at = first = 0
    for call, count in enumerate(counts):
        cols = count * LANES
        for i, out in enumerate((q_out, k_out, v_out)):
            out[:, at : at + cols] = (late if call else early)[:, first + i * cols : first + (i + 1) * cols]
        at += cols
        first = first + 3 * cols if call else 0
    rows = vectors[0].shape[0]
    half = inner_out.shape[0] // 2
    for i, out in enumerate(vectors):
        out[...] = late[i, first : first + rows]
    inner_out[0:half] = late[8, first : first + half]
    inner_out[half:] = late[16, first : first + half]
    table_out[...] = late[9, first : first + table_out.shape[0]]


def feed_columns_kernel(first, second, early, inner_out, outer_out, w_out, *, moves):
    rows, width = w_out.shape
    half = inner_out.shape[1] // 2
    both = jnp.concatenate([first[:, 0:half], second[:, 0:half]], axis=1)
    inner_out[...] = moved_lanes(both, moves)
    for part, value in enumerate((first, second)):
        for i in range(2):
            at = (2 * part + i) * rows
            outer_out[at : at + rows, :] = value[:, half + i * width : half + (i + 1) * width]
    w_out[...] = early[:, early.shape[1] - width :]


def small_blocks(core, place, vecs, inner, grows, bucket_rev, send, keep, columns, rows_d, rows_ff):
    n = len(place)
    span = bucket_rev.shape[1]
    row = lax.broadcasted_iota(jnp.int32, (8, LANES), 0)
    lane = lax.broadcasted_iota(jnp.int32, (8, LANES), 1)
    each = LANES // HEADS
    big = [jnp.where(bucket_rev[1:2, :] == m, grows, 0.0) for m in range(each)]
    big = jnp.concatenate(big + [jnp.zeros((LANES - each * HEADS, span), F32)], axis=0)
    high = big.astype(BF16)
    low = (big - high.astype(F32)).astype(BF16)
    hot = jnp.where(lax.broadcasted_iota(jnp.int32, (n, span), 0) == bucket_rev[0:1, :], 1.0, 0.0).astype(BF16)
    table = nt(hot, high) + nt(hot, low)

    def cut(value, at, count):
        tile, shift = at // LANES, at % LANES
        out = value[:, tile * LANES : (tile + 1) * LANES]
        if shift:
            out = pltpu.roll(out, LANES - shift, 1)
            if shift + count > LANES:
                more = pltpu.roll(value[:, (tile + 1) * LANES : (tile + 2) * LANES], LANES - shift, 1)
                out = jnp.where(lane < LANES - shift, out, more)
        return jnp.where(lane < count, out, 0.0)

    half = rows_ff // 2
    blocks = []
    for d in range(n):
        low_rows = jnp.where(row == 0, cut(inner, d * half, half), 0.0)
        low_rows = jnp.where(row == 1, table[d : d + 1], low_rows)
        last_rows = jnp.where(row == 0, cut(inner, (n + d) * half, half), 0.0)
        block = [cut(vecs, d * rows_d, rows_d), low_rows, last_rows]
        block += [jnp.zeros((rows_d - 24, LANES), F32)] * (rows_d > 24)
        blocks.append(jnp.concatenate(block, axis=0))
    put_blocks(core, place, blocks, send, keep, columns)


def attend_back_kernel(
    meta, q, k, v, lse, ctx, gctx, bias_rev, nin, frames, gatt, gin, w, vec, *refs, crossed, rows_d, counts, count,
):
    first = 2 * sum(counts)
    last = first + 2 * count == HEADS
    if last and crossed:
        gvec2, gb_inner, bucket_rev, *refs = refs
        before = [(refs[2 * i], refs[2 * i + 1], c) for i, c in enumerate(counts)]
        refs = refs[2 * len(counts) :]
    send, keep, gin_out, gvec_out, grow_out, base, gbase, delta_t, kt, dqkv, gk, gv, masks = refs
    rows, width = frames.shape
    unit = rows // UNITS
    window = rows - unit
    head = width // HEADS
    core = meta[5]
    place = [meta[6 + 2 * len(crossed) + i] for i in range(2 * len(crossed))]
    prod = gctx[...].astype(F32) * ctx[...].astype(F32)
    sel_row = lax.broadcasted_iota(jnp.int32, (16, width), 0)
    sel_col = lax.broadcasted_iota(jnp.int32, (16, width), 1)
    sel = jnp.where((sel_col >= sel_row * head) & (sel_col < (sel_row + 1) * head), 1.0, 0.0).astype(BF16)
    high = prod.astype(BF16)
    low = (prod - high.astype(F32)).astype(BF16)
    deltas = nt(sel, high) + nt(sel, low)
    for h in range(HEADS):
        delta_t[h] = deltas[h : h + 1]
    ranges = put_masks(meta, masks)
    lane = lax.broadcasted_iota(jnp.int32, (unit, LANES), 1)
    sub_lane = lax.broadcasted_iota(jnp.int32, (LANES, unit), 0)
    span = count * LANES

    def pair(step, carry):
        hp = first // 2 + step
        cols = pl.ds(pl.multiple_of(hp * LANES, LANES), LANES)
        here = pl.multiple_of(step * LANES, LANES)
        kt[...] = jnp.transpose(k[:, cols])
        gk[...] = jnp.zeros_like(gk)
        gv[...] = jnp.zeros_like(gv)
        gbase[...] = jnp.zeros_like(gbase)
        for sub in range(2):
            base[sub] = skewed(bias_rev[pl.ds(2 * hp + sub, 1), :], unit)
        for u in range(UNITS):
            ws = pl.multiple_of(ranges[u], LANES)
            win = pl.ds(ws, window)
            urows = slice(u * unit, (u + 1) * unit)
            mask = jnp.concatenate([masks[u], masks[u]], axis=1)
            kk = k[win, cols]
            vv = v[win, cols]
            qu = q[urows, cols]
            gu = gctx[urows, cols]
            offsets = [
                pl.ds(pl.multiple_of((rows - unit) + u * unit - ws - jb * unit, LANES), unit) for jb in range(UNITS - 1)
            ]
            qs = apart_heads(qu, lane, head)
            gs = apart_heads(gu, lane, head)
            rel = jnp.concatenate([jnp.concatenate([base[sub, :, o] for o in offsets], axis=0) for sub in range(2)], axis=1)
            lses = jnp.concatenate([lse[2 * hp + sub, :, urows] for sub in range(2)], axis=1)
            deltas = jnp.concatenate([delta_t[2 * hp + sub, :, urows] for sub in range(2)], axis=1)
            p = jnp.exp(nt(kk, qs) + rel + mask - lses)
            ds = (p * (nt(vv, gs) - deltas)).astype(BF16)
            gv[win, :] += nn(p.astype(BF16), gs)
            gk[win, :] += nn(ds, qs)
            gq = nn(kt[:, win], ds)
            d32 = ds.astype(F32)
            for sub in range(2):
                for jb, o in enumerate(offsets):
                    gbase[sub, :, o] += d32[jb * unit : (jb + 1) * unit, sub * unit : (sub + 1) * unit]
            gq_t = jnp.where(sub_lane < head, gq[:, :unit], gq[:, unit:])
            dqkv[urows, pl.ds(here, LANES)] = jnp.transpose(gq_t).astype(BF16) * BF16(head**-0.5)
        dqkv[:, pl.ds(span + here, LANES)] = gk[...].astype(BF16)
        dqkv[:, pl.ds(2 * span + here, LANES)] = gv[...].astype(BF16)
        for sub in range(2):
            grow_out[pl.ds(2 * step + sub, 1), :] = unskewed_sum(gbase[sub], unit)
        return carry

    grow_out[...] = jnp.zeros_like(grow_out)
    lax.fori_loop(0, count, pair, 0)
    at_columns = first * head
    grad_in = gin[...] if first else jnp.zeros((rows, width), F32)
    for part in range(3):
        d = dqkv[:, part * span : (part + 1) * span]
        grad_in = grad_in + nt(d, weight(w, slice(part * width + at_columns, part * width + at_columns + span)))
    grads = [(tn(nin[...], dqkv[...]), slice(0, 3 * span))]
    if first == 0:
        grads.append((tn(ctx[...], gatt[...].astype(BF16)), slice(3 * span, 3 * span + width)))
    for g, columns in grads:
        if crossed:
            put_blocks(core, place, row_blocks(g, rows_d), send, keep, columns)
        else:
            keep[:, columns] = g.astype(BF16)
    sums = [jnp.sum(dqkv[:, at : at + span].astype(F32), axis=0, keepdims=True) for at in (0, 2 * span)]
    gvec_out[...] = jnp.zeros_like(gvec_out)
    gvec_out[2:4, 0:span] = jnp.concatenate(sums, axis=0)
    if not last:
        gin_out[...] = grad_in
        return
    n, r = normalise(frames[...].astype(F32))
    gin_out[...] = (gatt[...] + norm_backward(n, r, vec[0:1, :], grad_in)).astype(BF16)
    gvec_out[0:1, :] = jnp.sum(grad_in * n, axis=0, keepdims=True)
    gvec_out[1:2, :] = jnp.sum(grad_in, axis=0, keepdims=True)
    if crossed:
        at = 0
        for vectors, _, c in before:
            gvec_out[2:4, at : at + c * LANES] = vectors[2:4, 0 : c * LANES]
            at += c * LANES
        gvec_out[2:4, at_columns : at_columns + span] = jnp.concatenate(sums, axis=0)
        gvec_out[4:8, :] = gvec2[0:4, :]
        grows = jnp.concatenate([grow[0 : 2 * c, :] for _, grow, c in before] + [grow_out[0 : 2 * count, :]], axis=0)
        small_blocks(
            core, place, gvec_out[...], jnp.broadcast_to(gb_inner[...], (8, gb_inner.shape[1])), grows, bucket_rev,
            send, keep, slice(3 * span, 3 * span + LANES), rows_d, gb_inner.shape[1] // len(place),
        )


def run_kernel(order, kernel, name, scalars, arrays, outs, scratch=(), spare=10, us=100, pin_in=True, pin_out=True, hbm_in=(), hbm_out=()):
    spec = pl.BlockSpec(memory_space=pltpu.VMEM)
    smem = pl.BlockSpec(memory_space=pltpu.SMEM)
    arrays = order.after(*arrays)
    arrays = [
        pltpu.with_memory_space_constraint(a, pltpu.VMEM if pin_in and i not in hbm_in else pltpu.HBM)
        for i, a in enumerate(arrays)
    ]
    limit = spare * MIB + sum(math.prod(b.shape) * jnp.dtype(b.dtype).itemsize for b in scratch)
    out = pl.pallas_call(
        kernel,
        in_specs=[smem] * len(scalars) + [spec] * len(arrays),
        out_specs=[spec] * len(outs),
        out_shape=[
            (pltpu.VMEM if pin_out and i not in hbm_out else jax.ShapeDtypeStruct)(s, d) for i, (s, d) in enumerate(outs)
        ],
        scratch_shapes=list(scratch),
        compiler_params=pltpu.CompilerParams(vmem_limit_bytes=limit),
        cost_estimate=pl.CostEstimate(flops=us * 1_000_000_000, bytes_accessed=us * 1_000_000, transcendentals=0),
        name=name,
    )(*scalars, *arrays)
    order.did(out[0])
    return out


def on_device(
    frames, ln1_gain, ln1_shift, w_query, b_query, w_key, w_value, b_value, w_out, b_out, ln2_gain, ln2_shift,
    w_inner, b_inner, w_outer, b_outer, bias_table, layout, valid, rel_index, cotangent, *, n,
):
    rows, width = frames.shape
    rows_d = w_query.shape[0]
    rows_ff = w_outer.shape[0]
    ff = w_inner.shape[1]
    span = rel_index.shape[0] + 1
    unit = rows // UNITS
    per_table = bias_table.shape[0]
    plan = plan_tables(n)
    core, chips, place = plan
    order = Order()
    direct = (
        rows_d % 8 == 0 and rows_d >= 24 and rows_ff == 4 * rows_d and max(rows_d, rows_ff, per_table) <= LANES and per_table % HEADS == 0
    )
    crossed = tuple(crossed_places(n)) if direct else ()
    crossed_outer = tuple(crossed_places(n, "outer")) if direct else ()
    unit_half = rows_ff // 2
    apart = [(d * rows_ff + h * unit_half, h * ff // 2 + d * unit_half, unit_half) for h in range(2) for d in range(n)]
    together = [(b, a, c) for a, b, c in apart]
    meta = [layout, valid.reshape(-1), core[None]]
    if direct:
        _, chips_outer, place_outer = plan_tables(n, "outer")
        meta += [chips, chips_outer, place, place_outer]
    meta = jnp.concatenate(meta).astype(jnp.int32)
    small_d = jnp.stack([ln1_gain, ln1_shift, b_query, b_value, b_out, ln2_gain, ln2_shift, b_outer])

    base = pltpu.VMEM((2, unit, span), F32)
    masks = pltpu.VMEM((UNITS, rows - unit, unit), F32)
    if direct:
        vectors = (ln1_gain, ln1_shift, b_query, b_value, b_out, ln2_gain, ln2_shift, b_outer, b_inner, bias_table)
        (part1,) = run_kernel(
            Order(), functools.partial(pack_first_kernel, rows_ff=rows_ff), "pack_first", [],
            [w_query, w_key, w_value, *(v[None] for v in vectors)], [((1, rows_d, 3 * width + LANES), BF16)],
            [pltpu.VMEM((rows_d, LANES), F32)], spare=4, pin_in=False,
        )
        g1 = Gather(part1, n, order)
        part2, part3 = run_kernel(
            order, functools.partial(pack_feed_kernel, moves=apart), "pack_feed", [], [w_inner, w_outer, w_out],
            [((1, rows_d, ff + width), BF16), ((1, rows_d, ff), BF16)], spare=4, pin_in=False,
        )
        g3 = Gather(part3, n, order, "outer")
        (part2,) = lax.optimization_barrier((part2, g1.got))[:1]
        g2 = Gather(part2, n, order)
        (g2.got,) = lax.optimization_barrier((g2.got, g3.got))[:1]
        for g in (g1, g1, g2, g1, g2, g3):
            g.step()
        (g2.got,) = lax.optimization_barrier((g2.got, g1.got))[:1]
        for g in (g2, g3):
            g.step()
        first = g1.finish()
        each = per_table // HEADS
        index = jnp.stack([rel_index // each, rel_index % each])
        bucket_rev = jnp.pad(index[:, ::-1], ((0, 6), (0, 1)), constant_values=-1)
        q, k, v, nin, w1, vec, inner_bias, bias_rev = run_kernel(
            order, functools.partial(project_kernel, crossed=crossed, rows_d=rows_d, rows_ff=rows_ff), "project", [meta],
            [frames, *first, bucket_rev],
            [((rows, width), BF16)] * 4
            + [((n // 2, 2 * rows_d, 3 * width), BF16), ((8, width), F32), ((1, ff), F32), ((16, span), F32)],
            [
                pltpu.VMEM((width // LANES + 1, 8, LANES), F32),
                pltpu.VMEM((ff // LANES + 1, 8, LANES), F32),
                pltpu.VMEM((n, LANES), F32),
            ],
            us=1, hbm_in=(0,),
        )
        chunk = [[((n // 2, rows_d, c), BF16)] * 2 for c in (ff, ff)]
        w_out_whole = [((n // 2, 2 * rows_d, width), BF16)]
        unpacked = [pltpu.VMEM((n // 2, 2 * rows_d, width), BF16), pltpu.VMEM((n // 2, rows_ff, width), BF16)]
    else:
        flat = jnp.concatenate([small_d.reshape(-1), b_inner, bias_table])
        per = flat.shape[0] // rows_d
        small = jnp.pad(flat.reshape(rows_d, per), ((0, 0), (0, LANES - per)))
        w1 = gathered(Gather(jnp.concatenate([w_query, w_key, w_value, small], axis=1), n, order).finish(), plan, n)
        w2 = (gathered(Gather(jnp.concatenate([w_inner, w_out], axis=1), n, order).finish(), plan, n),)
        w2 += (gathered(Gather(w_outer, n, order).finish(), plan, n),)
        flats = w1[:, 3 * width : 3 * width + per].reshape(n, rows_d * per)
        vec = flats[:, : 8 * rows_d].reshape(n, 8, rows_d).transpose(1, 0, 2).reshape(8, width).astype(F32)
        inner_bias = flats[:, 8 * rows_d : 8 * rows_d + rows_ff].reshape(1, ff).astype(F32)
        table = jnp.pad(flats[:, 8 * rows_d + rows_ff :].reshape(-1, HEADS), ((0, 0), (0, 16 - HEADS)))
        index_rev = jnp.pad(rel_index[::-1], (0, 1), constant_values=-1)
        ids = jnp.arange(table.shape[0], dtype=jnp.int32)[:, None]
        bias_rev = tn(table, (ids == index_rev[None]).astype(BF16))
        q, k, v, nin = run_kernel(
            order, project_body, "project", [meta], [frames, w1, vec], [((rows, width), BF16)] * 4
        )
        chunk = [[((8, LANES), BF16), ((c, max(width, ff // 2), max(width, ff // 2)), BF16)] for c in (2, 2)]
        w_out_whole = []
        unpacked = []

    ctx, lse = run_kernel(
        order, attend_kernel, "attend", [meta], [q, k, v, bias_rev],
        [((rows, width), BF16), ((HEADS, 1, rows), F32)], [base, pltpu.VMEM((LANES, rows), BF16), masks], spare=4, us=1,
    )

    def start(send, keep, scatter):
        return scatter.add(*((send, keep) if direct else split_natural(keep, plan, n)))

    if direct:
        g3.step()
        w2 = g2.finish()
    att, nmid, acc, gmid, gb1, send1, keep1, *w_out_all = run_kernel(
        order, functools.partial(feed_first_kernel, crossed=crossed, rows_d=rows_d), "feed_first", [meta],
        [frames, ctx, vec, inner_bias, cotangent, *w2],
        [((rows, width), F32), ((rows, width), BF16), ((rows, width), F32), ((rows, width), F32), ((1, ff // 2), F32)]
        + chunk[0] + w_out_whole,
        unpacked, spare=12,
    )
    if direct:
        w3 = g3.finish()
        begin = functools.partial(Scatter, n, order)
        sum_1 = begin("outer").add(send1, keep1)
    else:
        w3 = w2
    mixed, gatt, gctx, send2, keep2, gb2, gvec2 = run_kernel(
        order, functools.partial(feed_second_kernel, crossed=crossed_outer, rows_d=rows_d), "feed_second", [meta],
        [att, nmid, acc, gmid, ctx, vec, inner_bias, cotangent, *w_out_all, *w3],
        [((rows, width), BF16), ((rows, width), F32), ((rows, width), BF16)] + chunk[1]
        + [((1, ff // 2), F32), ((8, width), F32)],
        [pltpu.VMEM((rows, width), F32)] * 2 + unpacked, spare=12, hbm_out=(0,),
    )
    gb_inner = jnp.concatenate([gb1, gb2], axis=1)
    if direct:
        sum_1.step(2)
        sum_2 = begin().add(send2, keep2)
    else:
        whole_inner = jnp.concatenate([keep1[0, :width, : ff // 2], keep2[0, :width, : ff // 2]], axis=1)
        whole_outer = jnp.concatenate([keep1[1, : ff // 2, :width], keep2[1, : ff // 2, :width]], axis=0)
        begin = functools.partial(Scatter, n, order)
        sum_1 = begin().add(*split_natural(whole_outer, plan, n))
        sum_2 = begin().add(*split_natural(whole_inner, plan, n))

    counts = COUNTS
    passed = gatt
    done, earlier = [], []
    sum_early, sum_late = begin(), begin()
    for call, count in enumerate(counts):
        cols = count * LANES
        last = call == len(counts) - 1
        wide = 3 * cols + LANES * (last and direct) + width * (call == 0)
        part = [((n // 2, rows_d, wide), BF16)] * 2 if direct else [((8, LANES), BF16), ((width, wide), BF16)]
        extra = [gvec2, gb_inner, bucket_rev] + [a for pair in earlier for a in pair] if last and direct else []
        send, keep, passed, gvec1, grow = run_kernel(
            order,
            functools.partial(
                attend_back_kernel, crossed=crossed, rows_d=rows_d, counts=counts[:call], count=count
            ),
            "attend_back", [meta],
            [q, k, v, lse, ctx, gctx, bias_rev, nin, frames, gatt, passed, w1, vec] + extra,
            part + [((rows, width), BF16 if last else F32), ((8, width), F32), ((8, span), F32)],
            [
                base, base,
                pltpu.VMEM((HEADS, 1, rows), F32),
                pltpu.VMEM((LANES, rows), BF16),
                pltpu.VMEM((rows, 3 * cols), BF16),
                pltpu.VMEM((rows, LANES), F32),
                pltpu.VMEM((rows, LANES), F32),
                masks,
            ],
            spare=10, hbm_out=(2,) if last else (),
        )
        earlier.append((gvec1, grow))
        start(send, keep, sum_late if call else sum_early)
        if call == 0:
            sum_1.step(2)
            sum_2.step()
    for each_sum in (sum_early, sum_1, sum_2, sum_late, sum_early, sum_1, sum_2, sum_late, sum_early, sum_2, sum_late, sum_early, sum_late):
        if each_sum.steps:
            each_sum.step()
    sum_1, sum_2, early, late = sum_1.finish(), sum_2.finish(), sum_early.finish(), sum_late.finish()
    if direct:
        grad_inner, grad_outer, grad_w_out = run_kernel(
            Order(), functools.partial(feed_columns_kernel, moves=together), "feed_columns", [], [sum_1, sum_2, early],
            [((rows_d, ff), F32), ((rows_ff, width), F32), ((rows_d, width), F32)], spare=4, pin_out=False,
        )
    else:
        grad_inner, grad_outer = sum_2[:, :ff], sum_1
        grad_w_out = early[:, 3 * LANES * counts[0] :]
    if direct:
        sum_q, sum_k, sum_v, sum_b_inner, sum_table, *vecs = run_kernel(
            Order(), functools.partial(columns_kernel, counts=counts), "columns", [], [early, late],
            [((rows_d, width), F32)] * 3 + [((rows_ff,), F32), ((per_table,), F32)] + [((rows_d,), F32)] * 8,
            spare=4, pin_out=False,
        )
    else:
        places = [3 * LANES * sum(counts[1:call]) for call in range(len(counts))]
        calls = list(zip([early] + [late] * len(counts[1:]), places, [c * LANES for c in counts]))
        sum_q, sum_k, sum_v = (
            jnp.concatenate([p[:, at + i * cols : at + (i + 1) * cols] for p, at, cols in calls], axis=1) for i in range(3)
        )
        hot_rev = (ids == index_rev[None]).astype(F32)
        grow = jnp.concatenate([g[: 2 * c] for (_, g), c in zip(earlier, counts)])
        gtable = lax.dot_general(
            hot_rev, grow, (((1,), (1,)), ((), ())), precision=lax.Precision.HIGHEST, preferred_element_type=F32
        )
        gbias = jnp.concatenate([g[2:4, : c * LANES] for (g, _), c in zip(earlier, counts)], axis=1)
        gsmall = jnp.concatenate([gvec1[0:2], gbias, gvec2[0:4]])
        gsmall = gsmall.reshape(8, n, rows_d).transpose(1, 0, 2).reshape(n, 8 * rows_d)
        gflat = jnp.concatenate([gsmall, gb_inner.reshape(n, rows_ff), gtable.reshape(n, -1)], axis=1)
        gflat = jnp.pad(gflat, ((0, 0), (0, -gflat.shape[1] % LANES))).astype(BF16)
        sum_flat = Scatter(n, order).add(*split_natural(gflat, plan, n)).finish()[0]
        vecs = sum_flat[: 8 * rows_d].reshape(8, rows_d)
        sum_b_inner = sum_flat[8 * rows_d : 8 * rows_d + rows_ff]
        sum_table = sum_flat[8 * rows_d + rows_ff : 8 * rows_d + rows_ff + per_table]
    return (
        mixed, passed, vecs[0], vecs[1], sum_q, vecs[2], sum_k, sum_v, vecs[3],
        grad_w_out, vecs[4], vecs[5], vecs[6], grad_inner, sum_b_inner, grad_outer, vecs[7], sum_table,
    )


def solution(mesh):
    row, two = P("dp"), P("dp", None)
    in_specs = (two, row, row, two, row, two, two, row, two, row, row, row, two, row, two, row, row, row, two, P(), two)
    out_specs = (two, two, row, row, two, row, two, two, row, two, row, row, row, two, row, two, row, row)
    return jax.shard_map(
        functools.partial(on_device, n=mesh.shape["dp"]),
        mesh=mesh, in_specs=in_specs, out_specs=out_specs, check_vma=False,
    )
```

profile of v0, /device:TPU:0, one launch (start us, length us, event | category | flops | bytes accessed | tf_op | source)
XLA Modules:
  0.0 187.2 jit_solution(8381959399094258354)
XLA Ops:
  1.6 4.0 %collective-permute-start = (bf16[1,24,2432]{2,1,0:T(8,128)(2,1)S(1)}, bf16[1,24,2432]{2,1,0:T(8,128)(2,1)S(1)}, u32[]{:S(2)}, u32[]{:S(2)}) collective-permute-start(bf16[1,24,2432]{2,1,0:T(8,128)(2,1)S(1)} %pack_first.1), channel_id=1, source_target_pairs={{0,16},{1,17},{2,18},{3,19},{4,20},{5,21},{6,22},{7,23},{8,24},{9,... | collective-permute-start | bytes 350216 | tf_op jit(solution)/shard_map/ppermute | solution.py:69
  6.8 4.5 %collective-permute-done = bf16[1,24,2432]{2,1,0:T(8,128)(2,1)S(1)} collective-permute-done((bf16[1,24,2432]{2,1,0:T(8,128)(2,1)S(1)}, bf16[1,24,2432]{2,1,0:T(8,128)(2,1)S(1)}, u32[]{:S(2)}, u32[]{:S(2)}) %collective-permute-start) | collective-permute-done | bytes 116768 | tf_op jit(solution)/shard_map/ppermute | solution.py:69
  12.2 3.4 %collective-permute-start.3 = (bf16[1,24,3840]{2,1,0:T(8,128)(2,1)S(1)}, bf16[1,24,3840]{2,1,0:T(8,128)(2,1)S(1)}, u32[]{:S(2)}, u32[]{:S(2)}) collective-permute-start(bf16[1,24,3840]{2,1,0:T(8,128)(2,1)S(1)} %get-tuple-element.249), channel_id=1, source_target_pairs={{0,16},{1,17},{2,18},{3,19},{4,20},{5,21},{6,22},{7,23},{8,24},{9,... | collective-permute-start | bytes 552968 | tf_op jit(solution)/shard_map/ppermute | solution.py:69
  17.1 3.7 %collective-permute-done.4 = bf16[1,24,3072]{2,1,0:T(8,128)(2,1)S(1)} collective-permute-done((bf16[1,24,3072]{2,1,0:T(8,128)(2,1)S(1)}, bf16[1,24,3072]{2,1,0:T(8,128)(2,1)S(1)}, u32[]{:S(2)}, u32[]{:S(2)}) %collective-permute-start.4) | collective-permute-done | bytes 147488 | tf_op jit(solution)/shard_map/ppermute | solution.py:69
  23.7 3.4 %collective-permute-start.6 = (bf16[2,24,3840]{2,1,0:T(8,128)(2,1)S(1)}, bf16[2,24,3840]{2,1,0:T(8,128)(2,1)S(1)}, u32[]{:S(2)}, u32[]{:S(2)}) collective-permute-start(bf16[2,24,3840]{2,1,0:T(8,128)(2,1)S(1)} %constant_dynamic-update-slice_fusion.4), channel_id=1, source_target_pairs={{0,8},{1,9},{2,10},{3,11},{4,12},{5,13},{6,14},{7,15},{8,0},{9,1},... | collective-permute-start | bytes 1105928 | tf_op jit(solution)/shard_map/ppermute | solution.py:75
  27.1 3.9 %collective-permute-done.2 = bf16[4,24,2432]{2,1,0:T(8,128)(2,1)S(1)} collective-permute-done((bf16[4,24,2432]{2,1,0:T(8,128)(2,1)S(1)}, bf16[4,24,2432]{2,1,0:T(8,128)(2,1)S(1)}, u32[]{:S(2)}, u32[]{:S(2)}) %collective-permute-start.2) | collective-permute-done | bytes 466976 | tf_op jit(solution)/shard_map/ppermute | solution.py:75
  32.4 2.7 %collective-permute-done.6 = bf16[2,24,3840]{2,1,0:T(8,128)(2,1)S(1)} collective-permute-done((bf16[2,24,3840]{2,1,0:T(8,128)(2,1)S(1)}, bf16[2,24,3840]{2,1,0:T(8,128)(2,1)S(1)}, u32[]{:S(2)}, u32[]{:S(2)}) %collective-permute-start.6) | collective-permute-done | bytes 368672 | tf_op jit(solution)/shard_map/ppermute | solution.py:75
  37.6 11.6 %collective-permute-done.8 = bf16[4,24,3840]{2,1,0:T(8,128)(2,1)S(1)} collective-permute-done((bf16[4,24,3840]{2,1,0:T(8,128)(2,1)S(1)}, bf16[4,24,3840]{2,1,0:T(8,128)(2,1)S(1)}, u32[]{:S(2)}, u32[]{:S(2)}) %collective-permute-start.8) | collective-permute-done | bytes 737312 | tf_op jit(solution)/shard_map/ppermute | solution.py:75
  49.1 3.5 %collective-permute-done.5.p1 = bf16[8,24,2432]{2,1,0:T(8,128)(2,1)S(1)} collective-permute-done((bf16[8,24,2432]{2,1,0:T(8,128)(2,1)S(1)}, bf16[8,24,2432]{2,1,0:T(8,128)(2,1)S(1)}, u32[]{:S(2)}, u32[]{:S(2)}) %collective-permute-start.5) | collective-permute-done | bytes 933920 | tf_op jit(solution)/shard_map/ppermute | solution.py:75
  57.5 2.4 %collective-permute-start.12 = (bf16[4,24,3072]{2,1,0:T(8,128)(2,1)S(1)}, bf16[4,24,3072]{2,1,0:T(8,128)(2,1)}, u32[]{:S(2)}, u32[]{:S(2)}) collective-permute-start(bf16[4,24,3072]{2,1,0:T(8,128)(2,1)S(1)} %constant_dynamic-update-slice_fusion.14), channel_id=1, source_target_pairs={{0,8},{1,9},{2,10},{3,11},{4,12},{5,13},{6,14},{7,15},{8,0},{9,1},... | collective-permute-start | bytes 1769480 | tf_op jit(solution)/shard_map/ppermute | solution.py:75
  61.1 4.4 %project.1 = (bf16[512,768]{1,0:T(8,128)(2,1)S(1)}, bf16[512,768]{1,0:T(8,128)(2,1)S(1)}, bf16[512,768]{1,0:T(8,128)(2,1)S(1)}, bf16[512,768]{1,0:T(8,128)(2,1)S...) custom-call(s32[102]{0:T(128)S(1)} %concatenate.33.meta, ...), custom_call_target="tpu_custom_call" | custom-call | flops 1000000000 | bytes 1000000 | tf_op jit(solution)/shard_map/project/pallas_call | solution.py:731
  65.6 8.5 %attend.1 = (bf16[512,768]{1,0:T(8,128)(2,1)S(1)}, f32[12,1,512]{2,1,0:T(1,128)S(1)}) custom-call(s32[102]{0:T(128)S(1)} %concatenate.33.meta, bf16[512,768]{1,0:T(8,128)(2,1)S(1)} %get-tuple-element.353.q, bf16[512,768]{1,0:T(8,128)(2,1)S(1)} %get-tuple-element.354.k, bf16[512,768]{1,0:T(8,128)(2,1)S(1)} %get-tuple-element.355.v, ...), custom_call_target="tpu_custom_call" | custom-call | flops 1000000000 | bytes 1000000 | tf_op jit(solution)/shard_map/attend/pallas_call | solution.py:731
  77.4 2.1 %collective-permute-done.14.refs_3_ = bf16[8,24,3840]{2,1,0:T(8,128)(2,1)S(1)} collective-permute-done((bf16[8,24,3840]{2,1,0:T(8,128)(2,1)}, bf16[8,24,3840]{2,1,0:T(8,128)(2,1)S(1)}, u32[]{:S(2)}, u32[]{:S(2)}) %collective-permute-start.14) | collective-permute-done | bytes 1474592 | tf_op jit(solution)/shard_map/ppermute | solution.py:83
  79.5 12.8 %feed_first.1 = (f32[512,768]{1,0:T(8,128)S(1)}, bf16[512,768]{1,0:T(8,128)(2,1)S(1)}, f32[512,768]{1,0:T(8,128)S(1)}, f32[512,768]{1,0:T(8,128)S(1)}, f32[1,153...) custom-call(s32[102]{0:T(128)S(1)} %concatenate.33.meta, ...), custom_call_target="tpu_custom_call" | custom-call | flops 99999997952 | bytes 100000000 | tf_op jit(solution)/shard_map/feed_first/pallas_call | solution.py:731
  92.9 2.3 %collective-permute-done.17.refs_4_ = bf16[8,24,3072]{2,1,0:T(8,128)(2,1)S(1)} collective-permute-done((bf16[8,24,3072]{2,1,0:T(8,128)(2,1)S(1)}, bf16[8,24,3072]{2,1,0:T(8,128)(2,1)S(1)}, u32[]{:S(2)}, u32[]{:S(2)}) %collective-permute-start.17) | collective-permute-done | bytes 1179680 | tf_op jit(solution)/shard_map/ppermute | solution.py:83
  95.2 13.2 %feed_second.1 = (bf16[512,768]{1,0:T(8,128)(2,1)}, f32[512,768]{1,0:T(8,128)S(1)}, bf16[512,768]{1,0:T(8,128)(2,1)S(1)}, bf16[16,24,3072]{2,1,0:T(8,128)(2,1)S(...) custom-call(s32[102]{0:T(128)S(1)} %concatenate.33.meta, ...), custom_call_target="tpu_custom_call" | custom-call | flops 99999997952 | bytes 100000000 | tf_op jit(solution)/shard_map/feed_second/pallas_call | solution.py:731
  111.9 10.5 %attend_back.2 = (bf16[16,24,1920]{2,1,0:T(8,128)(2,1)S(1)}, bf16[16,24,1920]{2,1,0:T(8,128)(2,1)S(1)}, f32[512,768]{1,0:T(8,128)S(1)}, f32[8,768]{1,0:T(8,128)S(1)}, f32[8,1024]{1,0:T(8,128)S(1)}) custom-call(s32[102]{0:T(128)S(1)} %concatenate.33.meta, bf16[512,768]{1,0:T(8,128)(2,1)S(1)} %copy-done.3, bf16[512,768]{1,0:T(8,128)(2,1)S(1)} %copy-done.5, ...), custom_call_target="tpu_custom_call" | custom-call | flops 99999997952 | bytes 100000000 | tf_op jit(solution)/shard_map/attend_back/pallas_call | solution.py:731
  122.8 2.9 %collective-permute-start.26 = (bf16[2,24,3072]{2,1,0:T(8,128)(2,1)S(1)}, bf16[2,24,3072]{2,1,0:T(8,128)(2,1)S(1)}, u32[]{:S(2)}, u32[]{:S(2)}) collective-permute-start(bf16[2,24,3072]{2,1,0:T(8,128)(2,1)S(1)} %add_convert_fusion.10), channel_id=1, source_target_pairs={{0,8},{1,9},{2,10},{3,11},{4,12},{5,13},{6,14},{7,15},{8,0},{9,1},... | collective-permute-start | bytes 884744 | tf_op jit(solution)/shard_map/ppermute | solution.py:119
  127.5 11.9 %attend_back.3 = (bf16[16,24,1280]{2,1,0:T(8,128)(2,1)S(1)}, bf16[16,24,1280]{2,1,0:T(8,128)(2,1)S(1)}, bf16[512,768]{1,0:T(8,128)(2,1)}, f32[8,768]{1,0:T(8,128)}, f32[8,1024]{1,0:T(8,128)}) custom-call(s32[102]{0:T(128)S(1)} %concatenate.33.meta, bf16[512,768]{1,0:T(8,128)(2,1)S(1)} %copy-done.3, bf16[512,768]{1,0:T(8,128)(2,1)S(1)} %copy-done.5, ...), custom_call_target="tpu_custom_call" | custom-call | flops 99999997952 | bytes 100000000 | tf_op jit(solution)/shard_map/attend_back/pallas_call | solution.py:731
  146.2 11.1 %collective-permute-done.22 = bf16[8,24,1920]{2,1,0:T(8,128)(2,1)S(1)} collective-permute-done((bf16[8,24,1920]{2,1,0:T(8,128)(2,1)S(1)}, bf16[8,24,1920]{2,1,0:T(8,128)(2,1)S(1)}, u32[]{:S(2)}, u32[]{:S(2)}) %collective-permute-start.22) | collective-permute-done | bytes 737312 | tf_op jit(solution)/shard_map/ppermute | solution.py:119
  157.5 2.2 %collective-permute-start.27 = (bf16[4,24,1920]{2,1,0:T(8,128)(2,1)S(1)}, bf16[4,24,1920]{2,1,0:T(8,128)(2,1)S(1)}, u32[]{:S(2)}, u32[]{:S(2)}) collective-permute-start(bf16[4,24,1920]{2,1,0:T(8,128)(2,1)S(1)} %add_convert_fusion.6), channel_id=1, source_target_pairs={{0,2},{1,5},{2,0},{3,7},{4,6},{5,1},{6,4},{7,3},{8,10},{9,13},{10,... | collective-permute-start | bytes 1105928 | tf_op jit(solution)/shard_map/ppermute | solution.py:119
  163.0 4.8 %collective-permute-done.28 = bf16[8,24,1280]{2,1,0:T(8,128)(2,1)S(1)} collective-permute-done((bf16[8,24,1280]{2,1,0:T(8,128)(2,1)S(1)}, bf16[8,24,1280]{2,1,0:T(8,128)(2,1)S(1)}, u32[]{:S(2)}, u32[]{:S(2)}) %collective-permute-start.28) | collective-permute-done | bytes 491552 | tf_op jit(solution)/shard_map/ppermute | solution.py:119
  171.8 2.4 %collective-permute-done.33 = bf16[4,24,1280]{2,1,0:T(8,128)(2,1)S(1)} collective-permute-done((bf16[4,24,1280]{2,1,0:T(8,128)(2,1)S(1)}, bf16[4,24,1280]{2,1,0:T(8,128)(2,1)S(1)}, u32[]{:S(2)}, u32[]{:S(2)}) %collective-permute-start.33) | collective-permute-done | bytes 245792 | tf_op jit(solution)/shard_map/ppermute | solution.py:119
  175.8 2.8 %collective-permute-done.32 = bf16[2,24,1920]{2,1,0:T(8,128)(2,1)S(1)} collective-permute-done((bf16[2,24,1920]{2,1,0:T(8,128)(2,1)S(1)}, bf16[2,24,1920]{2,1,0:T(8,128)(2,1)S(1)}, u32[]{:S(2)}, u32[]{:S(2)}) %collective-permute-start.32) | collective-permute-done | bytes 184352 | tf_op jit(solution)/shard_map/ppermute | solution.py:119
  (152 shorter events, 50.0 us)
Async XLA Ops:
  23.7 11.4 %collective-permute-start.6 = (bf16[2,24,3840]{2,1,0:T(8,128)(2,1)S(1)}, bf16[2,24,3840]{2,1,0:T(8,128)(2,1)S(1)}, u32[]{:S(2)}, u32[]{:S(2)}) collective-permute-start(bf16[2,24,3840]{2,1,0:T(8,128)(2,1)S(1)} %constant_dynamic-update-slice_fusion.4), channel_id=1, source_target_pairs={{0,8},{1,9},{2,10},{3,11},{4,12},{5,13},{6,14},{7,15},{8,0},{9,1},... | collective-permute-start | bytes 1105928 | tf_op jit(solution)/shard_map/ppermute | solution.py:75
  31.1 21.5 %collective-permute-start.5 = (bf16[8,24,2432]{2,1,0:T(8,128)(2,1)S(1)}, bf16[8,24,2432]{2,1,0:T(8,128)(2,1)S(1)}, u32[]{:S(2)}, u32[]{:S(2)}) collective-permute-start(bf16[8,24,2432]{2,1,0:T(8,128)(2,1)S(1)} %constant_dynamic-update-slice_fusion.6.p0), channel_id=1, source_target_pairs={{0,4},{1,3},{2,6},{3,1},{4,0},{5,7},{6,2},{7,5},{8,12},{9,11},{10,... | collective-permute-start | bytes 2801672 | tf_op jit(solution)/shard_map/ppermute | solution.py:75
  35.2 14.0 %collective-permute-start.8 = (bf16[4,24,3840]{2,1,0:T(8,128)(2,1)S(1)}, bf16[4,24,3840]{2,1,0:T(8,128)(2,1)S(1)}, u32[]{:S(2)}, u32[]{:S(2)}) collective-permute-start(bf16[4,24,3840]{2,1,0:T(8,128)(2,1)S(1)} %constant_dynamic-update-slice_fusion.8), channel_id=1, source_target_pairs={{0,2},{1,5},{2,0},{3,7},{4,6},{5,1},{6,4},{7,3},{8,10},{9,13},{10,... | collective-permute-start | bytes 2211848 | tf_op jit(solution)/shard_map/ppermute | solution.py:75
  36.7 24.3 %collective-permute-start.9 = (bf16[8,24,2432]{2,1,0:T(8,128)(2,1)S(1)}, bf16[8,24,2432]{2,1,0:T(8,128)(2,1)S(1)}, u32[]{:S(2)}, u32[]{:S(2)}) collective-permute-start(bf16[8,24,2432]{2,1,0:T(8,128)(2,1)S(1)} %constant_dynamic-update-slice_fusion.6.p0), channel_id=1, source_target_pairs={{0,1},{1,0},{2,3},{3,2},{4,5},{5,4},{6,7},{7,6},{8,9},{9,8},{10,11... | collective-permute-start | bytes 2801672 | tf_op jit(solution)/shard_map/ppermute | solution.py:83
  36.8 17.7 %collective-permute-start.7 = (bf16[2,24,3072]{2,1,0:T(8,128)(2,1)S(1)}, bf16[2,24,3072]{2,1,0:T(8,128)(2,1)S(1)}, u32[]{:S(2)}, u32[]{:S(2)}) collective-permute-start(bf16[2,24,3072]{2,1,0:T(8,128)(2,1)S(1)} %constant_dynamic-update-slice_fusion.10), channel_id=1, source_target_pairs={{0,16},{1,17},{2,18},{3,19},{4,20},{5,21},{6,22},{7,23},{8,24},{9,... | collective-permute-start | bytes 884744 | tf_op jit(solution)/shard_map/ppermute | solution.py:75
  54.6 20.8 %collective-permute-start.11 = (bf16[8,24,3840]{2,1,0:T(8,128)(2,1)}, bf16[8,24,3840]{2,1,0:T(8,128)(2,1)}, u32[]{:S(2)}, u32[]{:S(2)}) collective-permute-start(bf16[8,24,3840]{2,1,0:T(8,128)(2,1)} %constant_dynamic-update-slice_fusion.12.refs_0_), channel_id=1, source_target_pairs={{0,4},{1,3},{2,6},{3,1},{4,0},{5,7},{6,2},{7,5},{8,12},{9,11},{10,... | collective-permute-start | bytes 4423688 | tf_op jit(solution)/shard_map/ppermute | solution.py:75
  57.5 16.7 %collective-permute-start.12 = (bf16[4,24,3072]{2,1,0:T(8,128)(2,1)S(1)}, bf16[4,24,3072]{2,1,0:T(8,128)(2,1)}, u32[]{:S(2)}, u32[]{:S(2)}) collective-permute-start(bf16[4,24,3072]{2,1,0:T(8,128)(2,1)S(1)} %constant_dynamic-update-slice_fusion.14), channel_id=1, source_target_pairs={{0,8},{1,9},{2,10},{3,11},{4,12},{5,13},{6,14},{7,15},{8,0},{9,1},... | collective-permute-start | bytes 1769480 | tf_op jit(solution)/shard_map/ppermute | solution.py:75
  60.2 17.2 %collective-permute-start.13 = (bf16[8,24,3840]{2,1,0:T(8,128)(2,1)}, bf16[8,24,3840]{2,1,0:T(8,128)(2,1)S(1)}, u32[]{:S(2)}, u32[]{:S(2)}) collective-permute-start(bf16[8,24,3840]{2,1,0:T(8,128)(2,1)} %constant_dynamic-update-slice_fusion.12.refs_0_), channel_id=1, source_target_pairs={{0,1},{1,0},{2,3},{3,2},{4,5},{5,4},{6,7},{7,6},{8,9},{9,8},{10,11... | collective-permute-start | bytes 4423688 | tf_op jit(solution)/shard_map/ppermute | solution.py:83
  75.7 17.2 %collective-permute-start.16 = (bf16[8,24,3072]{2,1,0:T(8,128)(2,1)S(1)}, bf16[8,24,3072]{2,1,0:T(8,128)(2,1)S(1)}, u32[]{:S(2)}, u32[]{:S(2)}) collective-permute-start(bf16[8,24,3072]{2,1,0:T(8,128)(2,1)S(1)} %constant_dynamic-update-slice_fusion.16.refs_1_), channel_id=1, source_target_pairs={{0,1},{1,0},{2,3},{3,2},{4,5},{5,4},{6,7},{7,6},{8,9},{9,8},{10,11... | collective-permute-start | bytes 3538952 | tf_op jit(solution)/shard_map/ppermute | solution.py:83
  76.0 16.3 %collective-permute-start.15 = (bf16[8,24,3072]{2,1,0:T(8,128)(2,1)S(1)}, bf16[8,24,3072]{2,1,0:T(8,128)(2,1)S(1)}, u32[]{:S(2)}, u32[]{:S(2)}) collective-permute-start(bf16[8,24,3072]{2,1,0:T(8,128)(2,1)S(1)} %constant_dynamic-update-slice_fusion.16.refs_1_), channel_id=1, source_target_pairs={{0,4},{1,3},{2,6},{3,1},{4,0},{5,7},{6,2},{7,5},{8,12},{9,11},{10,... | collective-permute-start | bytes 3538952 | tf_op jit(solution)/shard_map/ppermute | solution.py:75
  92.5 16.1 %collective-permute-start.18 = (bf16[16,24,3072]{2,1,0:T(8,128)(2,1)S(1)}, bf16[16,24,3072]{2,1,0:T(8,128)(2,1)S(1)}, u32[]{:S(2)}, u32[]{:S(2)}) collective-permute-start(bf16[16,24,3072]{2,1,0:T(8,128)(2,1)S(1)} %get-tuple-element.318), channel_id=1, source_target_pairs={{0,1},{1,0},{2,3},{3,2},{4,5},{5,4},{6,7},{7,6},{8,9},{9,8},{10,11... | collective-permute-start | bytes 7077896 | tf_op jit(solution)/shard_map/ppermute | solution.py:97
  108.4 17.4 %collective-permute-start.19 = (bf16[16,24,3072]{2,1,0:T(8,128)(2,1)S(1)}, bf16[16,24,3072]{2,1,0:T(8,128)(2,1)S(1)}, u32[]{:S(2)}, u32[]{:S(2)}) collective-permute-start(bf16[16,24,3072]{2,1,0:T(8,128)(2,1)S(1)} %get-tuple-element.343), channel_id=1, source_target_pairs={{0,1},{1,0},{2,3},{3,2},{4,5},{5,4},{6,7},{7,6},{8,9},{9,8},{10,11... | collective-permute-start | bytes 7077896 | tf_op jit(solution)/shard_map/ppermute | solution.py:97
  108.8 13.8 %collective-permute-start.20 = (bf16[4,24,3072]{2,1,0:T(8,128)(2,1)S(1)}, bf16[4,24,3072]{2,1,0:T(8,128)(2,1)S(1)}, u32[]{:S(2)}, u32[]{:S(2)}) collective-permute-start(bf16[4,24,3072]{2,1,0:T(8,128)(2,1)S(1)} %add_convert_fusion.4), channel_id=1, source_target_pairs={{0,4},{1,3},{2,6},{3,1},{4,0},{5,7},{6,2},{7,5},{8,12},{9,11},{10,... | collective-permute-start | bytes 1769480 | tf_op jit(solution)/shard_map/ppermute | solution.py:119
  111.1 29.0 %collective-permute-start.25 = (bf16[4,24,3072]{2,1,0:T(8,128)(2,1)}, bf16[4,24,3072]{2,1,0:T(8,128)(2,1)}, u32[]{:S(2)}, u32[]{:S(2)}) collective-permute-start(bf16[4,24,3072]{2,1,0:T(8,128)(2,1)} %add_convert_fusion.3), channel_id=1, source_target_pairs={{0,4},{1,3},{2,6},{3,1},{4,0},{5,7},{6,2},{7,5},{8,12},{9,11},{10,... | collective-permute-start | bytes 1769480 | tf_op jit(solution)/shard_map/ppermute | solution.py:119
  122.5 17.0 %collective-permute-start.21 = (bf16[16,24,1920]{2,1,0:T(8,128)(2,1)S(1)}, bf16[16,24,1920]{2,1,0:T(8,128)(2,1)S(1)}, u32[]{:S(2)}, u32[]{:S(2)}) collective-permute-start(bf16[16,24,1920]{2,1,0:T(8,128)(2,1)S(1)} %get-tuple-element.344), channel_id=1, source_target_pairs={{0,1},{1,0},{2,3},{3,2},{4,5},{5,4},{6,7},{7,6},{8,9},{9,8},{10,11... | collective-permute-start | bytes 4423688 | tf_op jit(solution)/shard_map/ppermute | solution.py:97
  122.8 18.8 %collective-permute-start.26 = (bf16[2,24,3072]{2,1,0:T(8,128)(2,1)S(1)}, bf16[2,24,3072]{2,1,0:T(8,128)(2,1)S(1)}, u32[]{:S(2)}, u32[]{:S(2)}) collective-permute-start(bf16[2,24,3072]{2,1,0:T(8,128)(2,1)S(1)} %add_convert_fusion.10), channel_id=1, source_target_pairs={{0,8},{1,9},{2,10},{3,11},{4,12},{5,13},{6,14},{7,15},{8,0},{9,1},... | collective-permute-start | bytes 884744 | tf_op jit(solution)/shard_map/ppermute | solution.py:119
  125.8 33.9 %collective-permute-start.30 = (bf16[2,24,3072]{2,1,0:T(8,128)(2,1)S(1)}, bf16[2,24,3072]{2,1,0:T(8,128)(2,1)S(1)}, u32[]{:S(2)}, u32[]{:S(2)}) collective-permute-start(bf16[2,24,3072]{2,1,0:T(8,128)(2,1)S(1)} %add_convert_fusion.9), channel_id=1, source_target_pairs={{0,8},{1,9},{2,10},{3,11},{4,12},{5,13},{6,14},{7,15},{8,0},{9,1},... | collective-permute-start | bytes 884744 | tf_op jit(solution)/shard_map/ppermute | solution.py:119
  126.3 16.5 %collective-permute-start.24 = (bf16[8,24,3072]{2,1,0:T(8,128)(2,1)S(1)}, bf16[8,24,3072]{2,1,0:T(8,128)(2,1)S(1)}, u32[]{:S(2)}, u32[]{:S(2)}) collective-permute-start(bf16[8,24,3072]{2,1,0:T(8,128)(2,1)S(1)} %add_convert_fusion), channel_id=1, source_target_pairs={{0,4},{1,3},{2,6},{3,1},{4,0},{5,7},{6,2},{7,5},{8,12},{9,11},{10,... | collective-permute-start | bytes 3538952 | tf_op jit(solution)/shard_map/ppermute | solution.py:119
  140.1 17.1 %collective-permute-start.22 = (bf16[8,24,1920]{2,1,0:T(8,128)(2,1)S(1)}, bf16[8,24,1920]{2,1,0:T(8,128)(2,1)S(1)}, u32[]{:S(2)}, u32[]{:S(2)}) collective-permute-start(bf16[8,24,1920]{2,1,0:T(8,128)(2,1)S(1)} %add_convert_fusion.1), channel_id=1, source_target_pairs={{0,4},{1,3},{2,6},{3,1},{4,0},{5,7},{6,2},{7,5},{8,12},{9,11},{10,... | collective-permute-start | bytes 2211848 | tf_op jit(solution)/shard_map/ppermute | solution.py:119
  142.7 17.0 %collective-permute-start.31 = (bf16[2,24,3072]{2,1,0:T(8,128)(2,1)S(1)}, bf16[2,24,3072]{2,1,0:T(8,128)(2,1)S(1)}, u32[]{:S(2)}, u32[]{:S(2)}) collective-permute-start(bf16[2,24,3072]{2,1,0:T(8,128)(2,1)S(1)} %add_convert_fusion.8), channel_id=1, source_target_pairs={{0,16},{1,17},{2,18},{3,19},{4,20},{5,21},{6,22},{7,23},{8,24},{9,... | collective-permute-start | bytes 884744 | tf_op jit(solution)/shard_map/ppermute | solution.py:119
  143.0 17.8 %collective-permute-start.29 = (bf16[4,24,3072]{2,1,0:T(8,128)(2,1)S(1)}, bf16[4,24,3072]{2,1,0:T(8,128)(2,1)S(1)}, u32[]{:S(2)}, u32[]{:S(2)}) collective-permute-start(bf16[4,24,3072]{2,1,0:T(8,128)(2,1)S(1)} %add_convert_fusion.2), channel_id=1, source_target_pairs={{0,2},{1,5},{2,0},{3,7},{4,6},{5,1},{6,4},{7,3},{8,10},{9,13},{10,... | collective-permute-start | bytes 1769480 | tf_op jit(solution)/shard_map/ppermute | solution.py:119
  145.2 22.6 %collective-permute-start.28 = (bf16[8,24,1280]{2,1,0:T(8,128)(2,1)S(1)}, bf16[8,24,1280]{2,1,0:T(8,128)(2,1)S(1)}, u32[]{:S(2)}, u32[]{:S(2)}) collective-permute-start(bf16[8,24,1280]{2,1,0:T(8,128)(2,1)S(1)} %add_convert_fusion.5), channel_id=1, source_target_pairs={{0,4},{1,3},{2,6},{3,1},{4,0},{5,7},{6,2},{7,5},{8,12},{9,11},{10,... | collective-permute-start | bytes 1474568 | tf_op jit(solution)/shard_map/ppermute | solution.py:119
  157.5 12.5 %collective-permute-start.27 = (bf16[4,24,1920]{2,1,0:T(8,128)(2,1)S(1)}, bf16[4,24,1920]{2,1,0:T(8,128)(2,1)S(1)}, u32[]{:S(2)}, u32[]{:S(2)}) collective-permute-start(bf16[4,24,1920]{2,1,0:T(8,128)(2,1)S(1)} %add_convert_fusion.6), channel_id=1, source_target_pairs={{0,2},{1,5},{2,0},{3,7},{4,6},{5,1},{6,4},{7,3},{8,10},{9,13},{10,... | collective-permute-start | bytes 1105928 | tf_op jit(solution)/shard_map/ppermute | solution.py:119
  160.7 21.3 %collective-permute-start.37 = (bf16[1,24,3072]{2,1,0:T(8,128)(2,1)S(1)}, bf16[1,24,3072]{2,1,0:T(8,128)(2,1)S(1)}, u32[]{:S(2)}, u32[]{:S(2)}) collective-permute-start(bf16[1,24,3072]{2,1,0:T(8,128)(2,1)S(1)} %add_convert_fusion.14), channel_id=1, source_target_pairs={{0,2},{1,5},{2,0},{3,7},{4,6},{5,1},{6,4},{7,3},{8,10},{9,13},{10,... | collective-permute-start | bytes 442376 | tf_op jit(solution)/shard_map/ppermute | solution.py:119
  (34 other events, 223.7 us)
where the time goes:
time: 188 us; the launch traced here: 187 us
  Pallas kernels  65.3 us (35%)
  waiting for transfers between devices  60.4 us (32%)
  starting transfers between devices  48.3 us (26%)
  other arithmetic  6.8 us (4%)
  local copies, waits for them, and re-layouts  4.35 us (2%)
  between operations  2.01 us (1%)
    pallas_call x10, Pallas kernels, run_kernel(): pl.pallas_call(kernel, in_specs=[smem] * len(scalars) + [spec] * len(arra...  65.3 us
    ppermute x18, waiting for transfers between devices, step(): lax.ppermute(out, 'dp', pairs(self.n, by_core))  24.6 us
    ppermute x9, waiting for transfers between devices, step(): self.got = lax.ppermute(self.held, 'dp', pairs(self.n, self.steps.pop(0)))  22.6 us
    ppermute x18, starting transfers between devices, step(): lax.ppermute(out, 'dp', pairs(self.n, by_core))  22.1 us
    ppermute x9, starting transfers between devices, step(): self.got = lax.ppermute(self.held, 'dp', pairs(self.n, self.steps.pop(0)))  14.3 us
    ppermute x3, starting transfers between devices, __init__(): self.got = lax.ppermute(self.held, 'dp', pairs(n, self.steps.pop(0)))  8.91 us
    ppermute x3, waiting for transfers between devices, __init__(): self.got = lax.ppermute(self.held, 'dp', pairs(n, self.steps.pop(0)))  8.79 us
    convert_element_type x18, other arithmetic, total(): out = out.astype(dtype)  5.3 us
  transfers between devices with their start and end apart: 40, of which 16 were waited for; matrix products, arithmetic and copies ran while one was open for 6% of the time, Pallas kernels for 34%

commit v1 on v0

--- a/solution.py
+++ b/solution.py
@@ -910,7 +910,7 @@
         earlier.append((gvec1, grow))
         start(send, keep, sum_late if call else sum_early)
         if call == 0:
-            sum_1.step(2)
+            sum_1.step()
             sum_2.step()
     for each_sum in (sum_early, sum_1, sum_2, sum_late, sum_early, sum_1, sum_2, sum_late, sum_early, sum_2, sum_late, sum_early, sum_late):
         if each_sum.steps:

time: 188 us -> 187 us (level)
  starting transfers between devices: 48.3 us -> 44.2 us
  waiting for transfers between devices: 60.4 us -> 64.3 us
    ppermute x18 -> x17, starting transfers between devices: 22.1 us -> 17.5 us  [step(): lax.ppermute(out, 'dp', pairs(self.n, by_core))]
    ppermute x18 -> x17, waiting for transfers between devices: 24.6 us -> 28.5 us  [step(): lax.ppermute(out, 'dp', pairs(self.n, by_core))]
    convert_element_type x18 -> x17, other arithmetic: 5.3 us -> 5.29 us  [total(): out = out.astype(dtype)]
  transfers between devices with their start and end apart: 40 -> 39, of which waited for: 16 -> 17; matrix products, arithmetic and copies ran while one was open for 6% -> 6% of each run, Pallas kernels for 34% -> 34%
where the time goes in v1:
time: 187 us
  Pallas kernels  65.3 us (35%)
  waiting for transfers between devices  64.3 us (34%)
  starting transfers between devices  44.2 us (24%)
  other arithmetic  6.8 us (4%)
  local copies, waits for them, and re-layouts  4.36 us (2%)
  between operations  2 us (1%)
    pallas_call x10, Pallas kernels, run_kernel(): pl.pallas_call(kernel, in_specs=[smem] * len(scalars) + [spec] * len(arra...  65.3 us
    ppermute x17, waiting for transfers between devices, step(): lax.ppermute(out, 'dp', pairs(self.n, by_core))  28.5 us
    ppermute x9, waiting for transfers between devices, step(): self.got = lax.ppermute(self.held, 'dp', pairs(self.n, self.steps.pop(0)))  22.6 us
    ppermute x17, starting transfers between devices, step(): lax.ppermute(out, 'dp', pairs(self.n, by_core))  17.5 us
    ppermute x9, starting transfers between devices, step(): self.got = lax.ppermute(self.held, 'dp', pairs(self.n, self.steps.pop(0)))  14.4 us
    ppermute x3, starting transfers between devices, __init__(): self.got = lax.ppermute(self.held, 'dp', pairs(n, self.steps.pop(0)))  8.91 us
    ppermute x3, waiting for transfers between devices, __init__(): self.got = lax.ppermute(self.held, 'dp', pairs(n, self.steps.pop(0)))  8.79 us
    convert_element_type x17, other arithmetic, total(): out = out.astype(dtype)  5.29 us
  transfers between devices with their start and end apart: 39, of which 17 were waited for; matrix products, arithmetic and copies ran while one was open for 6% of the time, Pallas kernels for 34%

profile of v1, /device:TPU:0, one launch (start us, length us, event | category | flops | bytes accessed | tf_op | source)
XLA Modules:
  0.0 186.9 jit_solution(1577381167895359588)
XLA Ops:
  1.6 4.0 %collective-permute-start = (bf16[1,24,2432]{2,1,0:T(8,128)(2,1)S(1)}, bf16[1,24,2432]{2,1,0:T(8,128)(2,1)S(1)}, u32[]{:S(2)}, u32[]{:S(2)}) collective-permute-start(bf16[1,24,2432]{2,1,0:T(8,128)(2,1)S(1)} %pack_first.1), channel_id=1, source_target_pairs={{0,16},{1,17},{2,18},{3,19},{4,20},{5,21},{6,22},{7,23},{8,24},{9,... | collective-permute-start | bytes 350216 | tf_op jit(solution)/shard_map/ppermute | solution.py:69
  6.8 4.5 %collective-permute-done = bf16[1,24,2432]{2,1,0:T(8,128)(2,1)S(1)} collective-permute-done((bf16[1,24,2432]{2,1,0:T(8,128)(2,1)S(1)}, bf16[1,24,2432]{2,1,0:T(8,128)(2,1)S(1)}, u32[]{:S(2)}, u32[]{:S(2)}) %collective-permute-start) | collective-permute-done | bytes 116768 | tf_op jit(solution)/shard_map/ppermute | solution.py:69
  12.2 3.4 %collective-permute-start.3 = (bf16[1,24,3840]{2,1,0:T(8,128)(2,1)S(1)}, bf16[1,24,3840]{2,1,0:T(8,128)(2,1)S(1)}, u32[]{:S(2)}, u32[]{:S(2)}) collective-permute-start(bf16[1,24,3840]{2,1,0:T(8,128)(2,1)S(1)} %get-tuple-element.246), channel_id=1, source_target_pairs={{0,16},{1,17},{2,18},{3,19},{4,20},{5,21},{6,22},{7,23},{8,24},{9,... | collective-permute-start | bytes 552968 | tf_op jit(solution)/shard_map/ppermute | solution.py:69
  17.1 3.7 %collective-permute-done.4 = bf16[1,24,3072]{2,1,0:T(8,128)(2,1)S(1)} collective-permute-done((bf16[1,24,3072]{2,1,0:T(8,128)(2,1)S(1)}, bf16[1,24,3072]{2,1,0:T(8,128)(2,1)S(1)}, u32[]{:S(2)}, u32[]{:S(2)}) %collective-permute-start.4) | collective-permute-done | bytes 147488 | tf_op jit(solution)/shard_map/ppermute | solution.py:69
  23.7 3.4 %collective-permute-start.6 = (bf16[2,24,3840]{2,1,0:T(8,128)(2,1)S(1)}, bf16[2,24,3840]{2,1,0:T(8,128)(2,1)S(1)}, u32[]{:S(2)}, u32[]{:S(2)}) collective-permute-start(bf16[2,24,3840]{2,1,0:T(8,128)(2,1)S(1)} %constant_dynamic-update-slice_fusion.4), channel_id=1, source_target_pairs={{0,8},{1,9},{2,10},{3,11},{4,12},{5,13},{6,14},{7,15},{8,0},{9,1},... | collective-permute-start | bytes 1105928 | tf_op jit(solution)/shard_map/ppermute | solution.py:75
  27.1 3.9 %collective-permute-done.2 = bf16[4,24,2432]{2,1,0:T(8,128)(2,1)S(1)} collective-permute-done((bf16[4,24,2432]{2,1,0:T(8,128)(2,1)S(1)}, bf16[4,24,2432]{2,1,0:T(8,128)(2,1)S(1)}, u32[]{:S(2)}, u32[]{:S(2)}) %collective-permute-start.2) | collective-permute-done | bytes 466976 | tf_op jit(solution)/shard_map/ppermute | solution.py:75
  32.4 2.7 %collective-permute-done.6 = bf16[2,24,3840]{2,1,0:T(8,128)(2,1)S(1)} collective-permute-done((bf16[2,24,3840]{2,1,0:T(8,128)(2,1)S(1)}, bf16[2,24,3840]{2,1,0:T(8,128)(2,1)S(1)}, u32[]{:S(2)}, u32[]{:S(2)}) %collective-permute-start.6) | collective-permute-done | bytes 368672 | tf_op jit(solution)/shard_map/ppermute | solution.py:75
  37.6 11.6 %collective-permute-done.8 = bf16[4,24,3840]{2,1,0:T(8,128)(2,1)S(1)} collective-permute-done((bf16[4,24,3840]{2,1,0:T(8,128)(2,1)S(1)}, bf16[4,24,3840]{2,1,0:T(8,128)(2,1)S(1)}, u32[]{:S(2)}, u32[]{:S(2)}) %collective-permute-start.8) | collective-permute-done | bytes 737312 | tf_op jit(solution)/shard_map/ppermute | solution.py:75
  49.1 3.5 %collective-permute-done.5.p1 = bf16[8,24,2432]{2,1,0:T(8,128)(2,1)S(1)} collective-permute-done((bf16[8,24,2432]{2,1,0:T(8,128)(2,1)S(1)}, bf16[8,24,2432]{2,1,0:T(8,128)(2,1)S(1)}, u32[]{:S(2)}, u32[]{:S(2)}) %collective-permute-start.5) | collective-permute-done | bytes 933920 | tf_op jit(solution)/shard_map/ppermute | solution.py:75
  57.5 2.4 %collective-permute-start.12 = (bf16[4,24,3072]{2,1,0:T(8,128)(2,1)S(1)}, bf16[4,24,3072]{2,1,0:T(8,128)(2,1)}, u32[]{:S(2)}, u32[]{:S(2)}) collective-permute-start(bf16[4,24,3072]{2,1,0:T(8,128)(2,1)S(1)} %constant_dynamic-update-slice_fusion.14), channel_id=1, source_target_pairs={{0,8},{1,9},{2,10},{3,11},{4,12},{5,13},{6,14},{7,15},{8,0},{9,1},... | collective-permute-start | bytes 1769480 | tf_op jit(solution)/shard_map/ppermute | solution.py:75
  61.1 4.4 %project.1 = (bf16[512,768]{1,0:T(8,128)(2,1)S(1)}, bf16[512,768]{1,0:T(8,128)(2,1)S(1)}, bf16[512,768]{1,0:T(8,128)(2,1)S(1)}, bf16[512,768]{1,0:T(8,128)(2,1)S...) custom-call(s32[102]{0:T(128)S(1)} %concatenate.33.meta, ...), custom_call_target="tpu_custom_call" | custom-call | flops 1000000000 | bytes 1000000 | tf_op jit(solution)/shard_map/project/pallas_call | solution.py:731
  65.6 8.5 %attend.1 = (bf16[512,768]{1,0:T(8,128)(2,1)S(1)}, f32[12,1,512]{2,1,0:T(1,128)S(1)}) custom-call(s32[102]{0:T(128)S(1)} %concatenate.33.meta, bf16[512,768]{1,0:T(8,128)(2,1)S(1)} %get-tuple-element.347.q, bf16[512,768]{1,0:T(8,128)(2,1)S(1)} %get-tuple-element.348.k, bf16[512,768]{1,0:T(8,128)(2,1)S(1)} %get-tuple-element.349.v, ...), custom_call_target="tpu_custom_call" | custom-call | flops 1000000000 | bytes 1000000 | tf_op jit(solution)/shard_map/attend/pallas_call | solution.py:731
  79.4 12.7 %feed_first.1 = (f32[512,768]{1,0:T(8,128)S(1)}, bf16[512,768]{1,0:T(8,128)(2,1)S(1)}, f32[512,768]{1,0:T(8,128)S(1)}, f32[512,768]{1,0:T(8,128)S(1)}, f32[1,153...) custom-call(s32[102]{0:T(128)S(1)} %concatenate.33.meta, ...), custom_call_target="tpu_custom_call" | custom-call | flops 99999997952 | bytes 100000000 | tf_op jit(solution)/shard_map/feed_first/pallas_call | solution.py:731
  92.8 2.3 %collective-permute-done.17.refs_4_ = bf16[8,24,3072]{2,1,0:T(8,128)(2,1)S(1)} collective-permute-done((bf16[8,24,3072]{2,1,0:T(8,128)(2,1)S(1)}, bf16[8,24,3072]{2,1,0:T(8,128)(2,1)S(1)}, u32[]{:S(2)}, u32[]{:S(2)}) %collective-permute-start.17) | collective-permute-done | bytes 1179680 | tf_op jit(solution)/shard_map/ppermute | solution.py:83
  95.1 13.2 %feed_second.1 = (bf16[512,768]{1,0:T(8,128)(2,1)}, f32[512,768]{1,0:T(8,128)S(1)}, bf16[512,768]{1,0:T(8,128)(2,1)S(1)}, bf16[16,24,3072]{2,1,0:T(8,128)(2,1)S(...) custom-call(s32[102]{0:T(128)S(1)} %concatenate.33.meta, ...), custom_call_target="tpu_custom_call" | custom-call | flops 99999997952 | bytes 100000000 | tf_op jit(solution)/shard_map/feed_second/pallas_call | solution.py:731
  111.8 10.5 %attend_back.2 = (bf16[16,24,1920]{2,1,0:T(8,128)(2,1)S(1)}, bf16[16,24,1920]{2,1,0:T(8,128)(2,1)S(1)}, f32[512,768]{1,0:T(8,128)S(1)}, f32[8,768]{1,0:T(8,128)S(1)}, f32[8,1024]{1,0:T(8,128)S(1)}) custom-call(s32[102]{0:T(128)S(1)} %concatenate.33.meta, bf16[512,768]{1,0:T(8,128)(2,1)S(1)} %copy-done.3, bf16[512,768]{1,0:T(8,128)(2,1)S(1)} %copy-done.5, ...), custom_call_target="tpu_custom_call" | custom-call | flops 99999997952 | bytes 100000000 | tf_op jit(solution)/shard_map/attend_back/pallas_call | solution.py:731
  123.3 2.5 %collective-permute-start.26 = (bf16[4,24,3072]{2,1,0:T(8,128)(2,1)S(1)}, bf16[4,24,3072]{2,1,0:T(8,128)(2,1)S(1)}, u32[]{:S(2)}, u32[]{:S(2)}) collective-permute-start(bf16[4,24,3072]{2,1,0:T(8,128)(2,1)S(1)} %add_convert_fusion.3), channel_id=1, source_target_pairs={{0,8},{1,9},{2,10},{3,11},{4,12},{5,13},{6,14},{7,15},{8,0},{9,1},... | collective-permute-start | bytes 1769480 | tf_op jit(solution)/shard_map/ppermute | solution.py:119
  127.4 11.9 %attend_back.3 = (bf16[16,24,1280]{2,1,0:T(8,128)(2,1)S(1)}, bf16[16,24,1280]{2,1,0:T(8,128)(2,1)S(1)}, bf16[512,768]{1,0:T(8,128)(2,1)}, f32[8,768]{1,0:T(8,128)}, f32[8,1024]{1,0:T(8,128)}) custom-call(s32[102]{0:T(128)S(1)} %concatenate.33.meta, bf16[512,768]{1,0:T(8,128)(2,1)S(1)} %copy-done.3, bf16[512,768]{1,0:T(8,128)(2,1)S(1)} %copy-done.5, ...), custom_call_target="tpu_custom_call" | custom-call | flops 99999997952 | bytes 100000000 | tf_op jit(solution)/shard_map/attend_back/pallas_call | solution.py:731
  146.1 11.1 %collective-permute-done.22 = bf16[8,24,1920]{2,1,0:T(8,128)(2,1)S(1)} collective-permute-done((bf16[8,24,1920]{2,1,0:T(8,128)(2,1)S(1)}, bf16[8,24,1920]{2,1,0:T(8,128)(2,1)S(1)}, u32[]{:S(2)}, u32[]{:S(2)}) %collective-permute-start.22) | collective-permute-done | bytes 737312 | tf_op jit(solution)/shard_map/ppermute | solution.py:119
  157.3 2.3 %collective-permute-start.27 = (bf16[4,24,1920]{2,1,0:T(8,128)(2,1)S(1)}, bf16[4,24,1920]{2,1,0:T(8,128)(2,1)S(1)}, u32[]{:S(2)}, u32[]{:S(2)}) collective-permute-start(bf16[4,24,1920]{2,1,0:T(8,128)(2,1)S(1)} %add_convert_fusion.7), channel_id=1, source_target_pairs={{0,2},{1,5},{2,0},{3,7},{4,6},{5,1},{6,4},{7,3},{8,10},{9,13},{10,... | collective-permute-start | bytes 1105928 | tf_op jit(solution)/shard_map/ppermute | solution.py:119
  161.3 6.4 %collective-permute-done.28 = bf16[8,24,1280]{2,1,0:T(8,128)(2,1)S(1)} collective-permute-done((bf16[8,24,1280]{2,1,0:T(8,128)(2,1)S(1)}, bf16[8,24,1280]{2,1,0:T(8,128)(2,1)S(1)}, u32[]{:S(2)}, u32[]{:S(2)}) %collective-permute-start.28) | collective-permute-done | bytes 491552 | tf_op jit(solution)/shard_map/ppermute | solution.py:119
  170.7 3.3 %collective-permute-done.32 = bf16[4,24,1280]{2,1,0:T(8,128)(2,1)S(1)} collective-permute-done((bf16[4,24,1280]{2,1,0:T(8,128)(2,1)S(1)}, bf16[4,24,1280]{2,1,0:T(8,128)(2,1)S(1)}, u32[]{:S(2)}, u32[]{:S(2)}) %collective-permute-start.32) | collective-permute-done | bytes 245792 | tf_op jit(solution)/shard_map/ppermute | solution.py:119
  174.8 2.7 %collective-permute-done.31 = bf16[2,24,1920]{2,1,0:T(8,128)(2,1)S(1)} collective-permute-done((bf16[2,24,1920]{2,1,0:T(8,128)(2,1)S(1)}, bf16[2,24,1920]{2,1,0:T(8,128)(2,1)S(1)}, u32[]{:S(2)}, u32[]{:S(2)}) %collective-permute-start.31) | collective-permute-done | bytes 184352 | tf_op jit(solution)/shard_map/ppermute | solution.py:119
  177.6 2.7 %collective-permute-done.37 = bf16[2,24,1280]{2,1,0:T(8,128)(2,1)S(1)} collective-permute-done((bf16[2,24,1280]{2,1,0:T(8,128)(2,1)S(1)}, bf16[2,24,1280]{2,1,0:T(8,128)(2,1)S(1)}, u32[]{:S(2)}, u32[]{:S(2)}) %collective-permute-start.37) | collective-permute-done | bytes 122912 | tf_op jit(solution)/shard_map/ppermute | solution.py:119
  (149 shorter events, 47.3 us)
Async XLA Ops:
  23.7 11.4 %collective-permute-start.6 = (bf16[2,24,3840]{2,1,0:T(8,128)(2,1)S(1)}, bf16[2,24,3840]{2,1,0:T(8,128)(2,1)S(1)}, u32[]{:S(2)}, u32[]{:S(2)}) collective-permute-start(bf16[2,24,3840]{2,1,0:T(8,128)(2,1)S(1)} %constant_dynamic-update-slice_fusion.4), channel_id=1, source_target_pairs={{0,8},{1,9},{2,10},{3,11},{4,12},{5,13},{6,14},{7,15},{8,0},{9,1},... | collective-permute-start | bytes 1105928 | tf_op jit(solution)/shard_map/ppermute | solution.py:75
  31.1 21.5 %collective-permute-start.5 = (bf16[8,24,2432]{2,1,0:T(8,128)(2,1)S(1)}, bf16[8,24,2432]{2,1,0:T(8,128)(2,1)S(1)}, u32[]{:S(2)}, u32[]{:S(2)}) collective-permute-start(bf16[8,24,2432]{2,1,0:T(8,128)(2,1)S(1)} %constant_dynamic-update-slice_fusion.6.p0), channel_id=1, source_target_pairs={{0,4},{1,3},{2,6},{3,1},{4,0},{5,7},{6,2},{7,5},{8,12},{9,11},{10,... | collective-permute-start | bytes 2801672 | tf_op jit(solution)/shard_map/ppermute | solution.py:75
  35.2 14.0 %collective-permute-start.8 = (bf16[4,24,3840]{2,1,0:T(8,128)(2,1)S(1)}, bf16[4,24,3840]{2,1,0:T(8,128)(2,1)S(1)}, u32[]{:S(2)}, u32[]{:S(2)}) collective-permute-start(bf16[4,24,3840]{2,1,0:T(8,128)(2,1)S(1)} %constant_dynamic-update-slice_fusion.8), channel_id=1, source_target_pairs={{0,2},{1,5},{2,0},{3,7},{4,6},{5,1},{6,4},{7,3},{8,10},{9,13},{10,... | collective-permute-start | bytes 2211848 | tf_op jit(solution)/shard_map/ppermute | solution.py:75
  36.7 24.4 %collective-permute-start.9 = (bf16[8,24,2432]{2,1,0:T(8,128)(2,1)S(1)}, bf16[8,24,2432]{2,1,0:T(8,128)(2,1)S(1)}, u32[]{:S(2)}, u32[]{:S(2)}) collective-permute-start(bf16[8,24,2432]{2,1,0:T(8,128)(2,1)S(1)} %constant_dynamic-update-slice_fusion.6.p0), channel_id=1, source_target_pairs={{0,1},{1,0},{2,3},{3,2},{4,5},{5,4},{6,7},{7,6},{8,9},{9,8},{10,11... | collective-permute-start | bytes 2801672 | tf_op jit(solution)/shard_map/ppermute | solution.py:83
  36.8 17.7 %collective-permute-start.7 = (bf16[2,24,3072]{2,1,0:T(8,128)(2,1)S(1)}, bf16[2,24,3072]{2,1,0:T(8,128)(2,1)S(1)}, u32[]{:S(2)}, u32[]{:S(2)}) collective-permute-start(bf16[2,24,3072]{2,1,0:T(8,128)(2,1)S(1)} %constant_dynamic-update-slice_fusion.10), channel_id=1, source_target_pairs={{0,16},{1,17},{2,18},{3,19},{4,20},{5,21},{6,22},{7,23},{8,24},{9,... | collective-permute-start | bytes 884744 | tf_op jit(solution)/shard_map/ppermute | solution.py:75
  54.6 20.8 %collective-permute-start.11 = (bf16[8,24,3840]{2,1,0:T(8,128)(2,1)}, bf16[8,24,3840]{2,1,0:T(8,128)(2,1)}, u32[]{:S(2)}, u32[]{:S(2)}) collective-permute-start(bf16[8,24,3840]{2,1,0:T(8,128)(2,1)} %constant_dynamic-update-slice_fusion.12.refs_0_), channel_id=1, source_target_pairs={{0,4},{1,3},{2,6},{3,1},{4,0},{5,7},{6,2},{7,5},{8,12},{9,11},{10,... | collective-permute-start | bytes 4423688 | tf_op jit(solution)/shard_map/ppermute | solution.py:75
  57.5 16.6 %collective-permute-start.12 = (bf16[4,24,3072]{2,1,0:T(8,128)(2,1)S(1)}, bf16[4,24,3072]{2,1,0:T(8,128)(2,1)}, u32[]{:S(2)}, u32[]{:S(2)}) collective-permute-start(bf16[4,24,3072]{2,1,0:T(8,128)(2,1)S(1)} %constant_dynamic-update-slice_fusion.14), channel_id=1, source_target_pairs={{0,8},{1,9},{2,10},{3,11},{4,12},{5,13},{6,14},{7,15},{8,0},{9,1},... | collective-permute-start | bytes 1769480 | tf_op jit(solution)/shard_map/ppermute | solution.py:75
  60.2 17.2 %collective-permute-start.13 = (bf16[8,24,3840]{2,1,0:T(8,128)(2,1)}, bf16[8,24,3840]{2,1,0:T(8,128)(2,1)S(1)}, u32[]{:S(2)}, u32[]{:S(2)}) collective-permute-start(bf16[8,24,3840]{2,1,0:T(8,128)(2,1)} %constant_dynamic-update-slice_fusion.12.refs_0_), channel_id=1, source_target_pairs={{0,1},{1,0},{2,3},{3,2},{4,5},{5,4},{6,7},{7,6},{8,9},{9,8},{10,11... | collective-permute-start | bytes 4423688 | tf_op jit(solution)/shard_map/ppermute | solution.py:83
  75.6 17.1 %collective-permute-start.16 = (bf16[8,24,3072]{2,1,0:T(8,128)(2,1)S(1)}, bf16[8,24,3072]{2,1,0:T(8,128)(2,1)S(1)}, u32[]{:S(2)}, u32[]{:S(2)}) collective-permute-start(bf16[8,24,3072]{2,1,0:T(8,128)(2,1)S(1)} %constant_dynamic-update-slice_fusion.16.refs_1_), channel_id=1, source_target_pairs={{0,1},{1,0},{2,3},{3,2},{4,5},{5,4},{6,7},{7,6},{8,9},{9,8},{10,11... | collective-permute-start | bytes 3538952 | tf_op jit(solution)/shard_map/ppermute | solution.py:83
  76.0 16.2 %collective-permute-start.15 = (bf16[8,24,3072]{2,1,0:T(8,128)(2,1)S(1)}, bf16[8,24,3072]{2,1,0:T(8,128)(2,1)S(1)}, u32[]{:S(2)}, u32[]{:S(2)}) collective-permute-start(bf16[8,24,3072]{2,1,0:T(8,128)(2,1)S(1)} %constant_dynamic-update-slice_fusion.16.refs_1_), channel_id=1, source_target_pairs={{0,4},{1,3},{2,6},{3,1},{4,0},{5,7},{6,2},{7,5},{8,12},{9,11},{10,... | collective-permute-start | bytes 3538952 | tf_op jit(solution)/shard_map/ppermute | solution.py:75
  92.4 16.1 %collective-permute-start.18 = (bf16[16,24,3072]{2,1,0:T(8,128)(2,1)S(1)}, bf16[16,24,3072]{2,1,0:T(8,128)(2,1)S(1)}, u32[]{:S(2)}, u32[]{:S(2)}) collective-permute-start(bf16[16,24,3072]{2,1,0:T(8,128)(2,1)S(1)} %get-tuple-element.315), channel_id=1, source_target_pairs={{0,1},{1,0},{2,3},{3,2},{4,5},{5,4},{6,7},{7,6},{8,9},{9,8},{10,11... | collective-permute-start | bytes 7077896 | tf_op jit(solution)/shard_map/ppermute | solution.py:97
  108.4 17.4 %collective-permute-start.19 = (bf16[16,24,3072]{2,1,0:T(8,128)(2,1)S(1)}, bf16[16,24,3072]{2,1,0:T(8,128)(2,1)S(1)}, u32[]{:S(2)}, u32[]{:S(2)}) collective-permute-start(bf16[16,24,3072]{2,1,0:T(8,128)(2,1)S(1)} %get-tuple-element.340), channel_id=1, source_target_pairs={{0,1},{1,0},{2,3},{3,2},{4,5},{5,4},{6,7},{7,6},{8,9},{9,8},{10,11... | collective-permute-start | bytes 7077896 | tf_op jit(solution)/shard_map/ppermute | solution.py:97
  108.8 14.3 %collective-permute-start.20 = (bf16[4,24,3072]{2,1,0:T(8,128)(2,1)S(1)}, bf16[4,24,3072]{2,1,0:T(8,128)(2,1)S(1)}, u32[]{:S(2)}, u32[]{:S(2)}) collective-permute-start(bf16[4,24,3072]{2,1,0:T(8,128)(2,1)S(1)} %add_convert_fusion.5), channel_id=1, source_target_pairs={{0,4},{1,3},{2,6},{3,1},{4,0},{5,7},{6,2},{7,5},{8,12},{9,11},{10,... | collective-permute-start | bytes 1769480 | tf_op jit(solution)/shard_map/ppermute | solution.py:119
  111.2 30.3 %collective-permute-start.25 = (bf16[4,24,3072]{2,1,0:T(8,128)(2,1)}, bf16[4,24,3072]{2,1,0:T(8,128)(2,1)}, u32[]{:S(2)}, u32[]{:S(2)}) collective-permute-start(bf16[4,24,3072]{2,1,0:T(8,128)(2,1)} %add_convert_fusion.4), channel_id=1, source_target_pairs={{0,4},{1,3},{2,6},{3,1},{4,0},{5,7},{6,2},{7,5},{8,12},{9,11},{10,... | collective-permute-start | bytes 1769480 | tf_op jit(solution)/shard_map/ppermute | solution.py:119
  122.4 17.4 %collective-permute-start.21 = (bf16[16,24,1920]{2,1,0:T(8,128)(2,1)S(1)}, bf16[16,24,1920]{2,1,0:T(8,128)(2,1)S(1)}, u32[]{:S(2)}, u32[]{:S(2)}) collective-permute-start(bf16[16,24,1920]{2,1,0:T(8,128)(2,1)S(1)} %get-tuple-element.341), channel_id=1, source_target_pairs={{0,1},{1,0},{2,3},{3,2},{4,5},{5,4},{6,7},{7,6},{8,9},{9,8},{10,11... | collective-permute-start | bytes 4423688 | tf_op jit(solution)/shard_map/ppermute | solution.py:97
  123.3 18.2 %collective-permute-start.26 = (bf16[4,24,3072]{2,1,0:T(8,128)(2,1)S(1)}, bf16[4,24,3072]{2,1,0:T(8,128)(2,1)S(1)}, u32[]{:S(2)}, u32[]{:S(2)}) collective-permute-start(bf16[4,24,3072]{2,1,0:T(8,128)(2,1)S(1)} %add_convert_fusion.3), channel_id=1, source_target_pairs={{0,8},{1,9},{2,10},{3,11},{4,12},{5,13},{6,14},{7,15},{8,0},{9,1},... | collective-permute-start | bytes 1769480 | tf_op jit(solution)/shard_map/ppermute | solution.py:119
  126.2 16.5 %collective-permute-start.24 = (bf16[8,24,3072]{2,1,0:T(8,128)(2,1)S(1)}, bf16[8,24,3072]{2,1,0:T(8,128)(2,1)S(1)}, u32[]{:S(2)}, u32[]{:S(2)}) collective-permute-start(bf16[8,24,3072]{2,1,0:T(8,128)(2,1)S(1)} %add_convert_fusion), channel_id=1, source_target_pairs={{0,4},{1,3},{2,6},{3,1},{4,0},{5,7},{6,2},{7,5},{8,12},{9,11},{10,... | collective-permute-start | bytes 3538952 | tf_op jit(solution)/shard_map/ppermute | solution.py:119
  140.0 17.1 %collective-permute-start.22 = (bf16[8,24,1920]{2,1,0:T(8,128)(2,1)S(1)}, bf16[8,24,1920]{2,1,0:T(8,128)(2,1)S(1)}, u32[]{:S(2)}, u32[]{:S(2)}) collective-permute-start(bf16[8,24,1920]{2,1,0:T(8,128)(2,1)S(1)} %add_convert_fusion.1), channel_id=1, source_target_pairs={{0,4},{1,3},{2,6},{3,1},{4,0},{5,7},{6,2},{7,5},{8,12},{9,11},{10,... | collective-permute-start | bytes 2211848 | tf_op jit(solution)/shard_map/ppermute | solution.py:119
  142.6 17.0 %collective-permute-start.30 = (bf16[2,24,3072]{2,1,0:T(8,128)(2,1)S(1)}, bf16[2,24,3072]{2,1,0:T(8,128)(2,1)S(1)}, u32[]{:S(2)}, u32[]{:S(2)}) collective-permute-start(bf16[2,24,3072]{2,1,0:T(8,128)(2,1)S(1)} %add_convert_fusion.9), channel_id=1, source_target_pairs={{0,16},{1,17},{2,18},{3,19},{4,20},{5,21},{6,22},{7,23},{8,24},{9,... | collective-permute-start | bytes 884744 | tf_op jit(solution)/shard_map/ppermute | solution.py:119
  142.9 17.7 %collective-permute-start.29 = (bf16[4,24,3072]{2,1,0:T(8,128)(2,1)S(1)}, bf16[4,24,3072]{2,1,0:T(8,128)(2,1)S(1)}, u32[]{:S(2)}, u32[]{:S(2)}) collective-permute-start(bf16[4,24,3072]{2,1,0:T(8,128)(2,1)S(1)} %add_convert_fusion.2), channel_id=1, source_target_pairs={{0,2},{1,5},{2,0},{3,7},{4,6},{5,1},{6,4},{7,3},{8,10},{9,13},{10,... | collective-permute-start | bytes 1769480 | tf_op jit(solution)/shard_map/ppermute | solution.py:119
  144.6 23.1 %collective-permute-start.28 = (bf16[8,24,1280]{2,1,0:T(8,128)(2,1)S(1)}, bf16[8,24,1280]{2,1,0:T(8,128)(2,1)S(1)}, u32[]{:S(2)}, u32[]{:S(2)}) collective-permute-start(bf16[8,24,1280]{2,1,0:T(8,128)(2,1)S(1)} %add_convert_fusion.6), channel_id=1, source_target_pairs={{0,4},{1,3},{2,6},{3,1},{4,0},{5,7},{6,2},{7,5},{8,12},{9,11},{10,... | collective-permute-start | bytes 1474568 | tf_op jit(solution)/shard_map/ppermute | solution.py:119
  157.3 12.0 %collective-permute-start.27 = (bf16[4,24,1920]{2,1,0:T(8,128)(2,1)S(1)}, bf16[4,24,1920]{2,1,0:T(8,128)(2,1)S(1)}, u32[]{:S(2)}, u32[]{:S(2)}) collective-permute-start(bf16[4,24,1920]{2,1,0:T(8,128)(2,1)S(1)} %add_convert_fusion.7), channel_id=1, source_target_pairs={{0,2},{1,5},{2,0},{3,7},{4,6},{5,1},{6,4},{7,3},{8,10},{9,13},{10,... | collective-permute-start | bytes 1105928 | tf_op jit(solution)/shard_map/ppermute | solution.py:119
  160.6 20.7 %collective-permute-start.36 = (bf16[1,24,3072]{2,1,0:T(8,128)(2,1)S(1)}, bf16[1,24,3072]{2,1,0:T(8,128)(2,1)S(1)}, u32[]{:S(2)}, u32[]{:S(2)}) collective-permute-start(bf16[1,24,3072]{2,1,0:T(8,128)(2,1)S(1)} %add_convert_fusion.13), channel_id=1, source_target_pairs={{0,2},{1,5},{2,0},{3,7},{4,6},{5,1},{6,4},{7,3},{8,10},{9,13},{10,... | collective-permute-start | bytes 442376 | tf_op jit(solution)/shard_map/ppermute | solution.py:119
  170.0 12.3 %collective-permute-start.35 = (bf16[1,24,3072]{2,1,0:T(8,128)(2,1)S(1)}, bf16[1,24,3072]{2,1,0:T(8,128)(2,1)S(1)}, u32[]{:S(2)}, u32[]{:S(2)}) collective-permute-start(bf16[1,24,3072]{2,1,0:T(8,128)(2,1)S(1)} %add_convert_fusion.12), channel_id=1, source_target_pairs={{0,16},{1,17},{2,18},{3,19},{4,20},{5,21},{6,22},{7,23},{8,24},{9,... | collective-permute-start | bytes 442376 | tf_op jit(solution)/shard_map/ppermute | solution.py:119
  (33 other events, 209.5 us)
